TPU v7x, 128 devices: a whole 4x4x4 slice. The times are simulated.
128 devices in a mesh: stretch: 32 (over x, z, core), space: 4 (over y).
Axes of the slice: x: 4, y: 4, z: 4, core: 2. Of those that a mesh axis runs over, the one named last changes fastest.
Arguments:
- frames: bfloat16 [128, 8, 32, 384], P('stretch', 'space')
- stretch_table: int32 [32, 4], P('stretch'), may hold values from -1 to 31, as said below
- conv_weight: bfloat16 [2, 3, 3, 3, 384, 384], replicated, may hold values from -0.0625 to 0.0625
- norm_gain: float32 [2, 384], replicated, may hold values from 0.5 to 1.5
- norm_bias: float32 [2, 384], replicated, may hold values from -3 to 3
- cotangent: bfloat16 [128, 8, 32, 384], P('stretch', 'space'), may hold values from -6 to 6
Outputs:
- block_output: bfloat16 [128, 8, 32, 384], P('stretch', 'space')
- input_grad: bfloat16 [128, 8, 32, 384], P('stretch', 'space')
Inputs may be any that keep to these rules, and one draw needn't show every extreme that they name: `stretch_table`: row d describes the stretch held at index d of the stretch axis: its clip's number, its position in the clip (0 at a clip's first stretch), the index that holds the clip's next stretch and the one that holds its previous stretch, -1 where there is none. A stretch's successor names it as its predecessor.
All inputs are finite; a program needn't handle non-finite values.
Results may differ from a plain program's by a relative error of at most 0.015.
Values may be sent and summed in bfloat16 or wider, within the bound.
No kernel may reach another device: no remote copies, remote signals or barrier semaphores. Data moves between devices by JAX's collectives and lax.ppermute only.
A program may use at most 128 MiB of HBM per device.

v0:
```python
import jax
import jax.numpy as jnp
from jax import lax
from jax.sharding import PartitionSpec as P

C = 384
GROUPS = 32
FRAMES = 4
LAYERS = 2


def with_halo(cells, sides, width):
    for axis, dim in sides:
        count = lax.axis_size(axis)
        ends = count - 1
        head = lax.slice_in_dim(cells, 0, width, axis=dim)
        tail = lax.slice_in_dim(cells, cells.shape[dim] - width, cells.shape[dim], axis=dim)
        cells = jnp.concatenate(
            [
                lax.ppermute(tail, axis, [(i, (i + 1) % count) for i in range(ends)]),
                cells,
                lax.ppermute(head, axis, [((i + 1) % count, i) for i in range(ends)]),
            ],
            axis=dim,
        )
    return cells


def group_totals(values):
    nframe = values.shape[0]
    per_chan = jnp.sum(values, axis=(1, 2))
    return jnp.sum(per_chan.reshape(nframe, GROUPS, C // GROUPS), axis=2)


def spread(values):
    return jnp.repeat(values, C // GROUPS, axis=1)[:, None, None, :]


def norm_forward(acts, gain_row, bias_row, cell_count):
    acts_f32 = acts.astype(jnp.float32)
    mean_val = lax.psum(group_totals(acts_f32), "space") / cell_count
    centered = acts_f32 - spread(mean_val)
    variance = lax.psum(group_totals(centered * centered), "space") / cell_count
    inv_std = lax.rsqrt(variance + 1e-05)
    normed = centered * spread(inv_std)
    activated = jax.nn.silu(normed * gain_row + bias_row).astype(jnp.bfloat16)
    return (activated, mean_val, inv_std)


def norm_backward(acts, mean_val, inv_std, gain_row, bias_row, upstream, cell_count):
    normed = (acts.astype(jnp.float32) - spread(mean_val)) * spread(inv_std)
    pre_act = normed * gain_row + bias_row
    sigmoid_val = jax.nn.sigmoid(pre_act)
    grad_normed = upstream * sigmoid_val * (1.0 + pre_act * (1.0 - sigmoid_val)) * gain_row
    first_sum, second_sum = lax.psum(
        (group_totals(grad_normed), group_totals(grad_normed * normed)), "space"
    )
    return spread(inv_std) * (
        grad_normed - spread(first_sum / cell_count) - normed * spread(second_sum / cell_count)
    )


def conv_forward(extended, kernel):
    row_ext = with_halo(extended, (("space", 1),), 1)
    padded = jnp.pad(row_ext, ((0, 0), (0, 0), (1, 1), (0, 0)))
    result = lax.conv_general_dilated(
        padded[None],
        kernel,
        (1, 1, 1),
        "VALID",
        dimension_numbers=("NDHWC", "DHWIO", "NDHWC"),
        preferred_element_type=jnp.float32,
    )
    return result[0]


def conv_adjoint(grad_out, flipped):
    padded = jnp.pad(grad_out, ((2, 2), (2, 2), (1, 1), (0, 0)))
    full_grad = lax.conv_general_dilated(
        padded[None],
        flipped,
        (1, 1, 1),
        "VALID",
        dimension_numbers=("NDHWC", "DHWIO", "NDHWC"),
        preferred_element_type=jnp.float32,
    )[0]
    edge_rows = jnp.stack([full_grad[:, 0], full_grad[:, -1]], axis=1)
    moved_rows = with_halo(edge_rows.astype(jnp.bfloat16), (("space", 1),), 1).astype(
        edge_rows.dtype
    )
    inner_rows = full_grad[:, 1:-1]
    inner_rows = inner_rows.at[:, 0].add(moved_rows[:, 0])
    inner_rows = inner_rows.at[:, -1].add(moved_rows[:, 3])
    return inner_rows


def chooser(owner, running, portion):
    width = portion.shape[0]
    matched = jnp.arange(width, dtype=jnp.int32) == owner
    picked = jnp.where(matched[:, None, None, None, None], portion, jnp.zeros((), portion.dtype))
    return running + jnp.sum(picked, axis=0).astype(running.dtype)


def per_device(frames, stretch_table, conv_weight, norm_gain, norm_bias, cotangent):
    source_dev = stretch_table[0, 3]
    target_dev = stretch_table[0, 2]
    row_count = frames.shape[1]
    col_count = frames.shape[2]
    cell_count = float(row_count * lax.axis_size("space") * col_count * (C // GROUPS))
    saved = []
    acts = frames
    for layer_idx in range(LAYERS):
        gain_row = norm_gain[layer_idx]
        bias_row = norm_bias[layer_idx]
        activated, mean_val, inv_std = norm_forward(acts, gain_row, bias_row, cell_count)
        saved.append((acts, mean_val, inv_std))
        empty = jnp.zeros((2, row_count, col_count, C), jnp.bfloat16)
        carried = chooser(
            source_dev,
            empty,
            lax.all_gather(activated[FRAMES - 2 :][None], "stretch", axis=0, tiled=True),
        )
        extended = jnp.concatenate([carried, activated], axis=0)
        acts = conv_forward(extended, conv_weight[layer_idx]).astype(jnp.bfloat16)
    grad_acts = cotangent
    for layer_idx in reversed(range(LAYERS)):
        flipped = jnp.swapaxes(jnp.flip(conv_weight[layer_idx], (0, 1, 2)), 3, 4)
        ext_grad = conv_adjoint(grad_acts, flipped)
        empty = jnp.zeros((2, row_count, col_count, C), jnp.float32)
        returned = chooser(
            target_dev,
            empty,
            jax.tree.map(
                lambda a: lax.all_gather(a, "stretch", axis=0, tiled=True),
                ext_grad[:2][None].astype(jnp.bfloat16),
            ).astype(jnp.float32),
        )
        upstream = ext_grad[2:].at[FRAMES - 2 :].add(returned)
        stored_acts, mean_val, inv_std = saved[layer_idx]
        grad_f32 = norm_backward(
            stored_acts,
            mean_val,
            inv_std,
            norm_gain[layer_idx],
            norm_bias[layer_idx],
            upstream,
            cell_count,
        )
        grad_acts = grad_f32.astype(jnp.bfloat16)
    return (acts, grad_acts)


def solution(mesh):
    in_specs = (
        P("stretch", "space", None, None),
        P("stretch", None),
        P(),
        P(),
        P(),
        P("stretch", "space", None, None),
    )
    out_specs = (P("stretch", "space", None, None), P("stretch", "space", None, None))
    return jax.shard_map(
        per_device, mesh=mesh, in_specs=in_specs, out_specs=out_specs, check_vma=False
    )
```

profile of v0, /device:TPU:0, one launch (start us, length us, event | category | flops | bytes accessed | tf_op | source)
XLA Modules:
  0.0 250.8 jit_solution(6025494179355601640)
XLA Ops:
  7.2 1.0 convert_reduce_fusion
  8.4 10.8 %psum.56 = f32[4,32]{1,0:T(4,128)S(1)} all-reduce(f32[4,32]{1,0:T(4,128)S(1)} %reduce_sum.187), channel_id=1, replica_groups=mesh['stretch'=32,'space'=4] {'space'}, use_global_device_ids=true, to_apply=%region_2.0 | all-reduce | flops 128 | bytes 1024 | tf_op jit(solution)/shard_map/psum | solution.py:41
  19.4 1.0 fusion.97
  20.6 7.7 %psum.57 = f32[4,32]{1,0:T(4,128)S(1)} all-reduce(f32[4,32]{1,0:T(4,128)S(1)} %reduce_sum.189), channel_id=1, replica_groups=mesh['stretch'=32,'space'=4] {'space'}, use_global_device_ids=true, to_apply=%region_5.0 | all-reduce | flops 128 | bytes 1024 | tf_op jit(solution)/shard_map/psum | solution.py:43
  28.6 0.8 slice_reduce_fusion.2
  29.4 1.1 fusion.89
  30.5 0.7 slice.312
  31.2 1.1 copy.55
  33.3 12.9 %fusion.36 = f32[6,4,8,5,384]{4,2,3,1,0:T(8,128)S(1)} fusion(bf16[2,3,3,3,384,384]{5,4,3,2,1,0:T(8,128)(2,1)} %param.20, bf16[8,6,1,7,2,384]{5,3,4,1,0,2:T(8,128)(2,1)S(1)} %slice.322, bf16[8,6,1,8,5,384]{5,3,4,1,0,2:T(8,128)(2,1)S(1)} %copy.57, pred[8,5]{0,1:T(8,128)(4,1)S(1)} %copy-done.2), kind=kOutput, calls=%fused_computation.39 | convolution fusion | flops 7650680832 | bytes 11427880 | tf_op jit(solution)/shard_map/conv_general_dilated | solution.py:79
  46.9 3.9 %collective-permute-start.4 = (bf16[6,1,32,384]{3,2,1,0:T(8,128)(2,1)S(1)}, bf16[6,1,32,384]{3,2,1,0:T(8,128)(2,1)S(1)}, u32[]{:S(2)}, u32[]{:S(2)}) collective-permute-start(bf16[6,1,32,384]{3,2,1,0:T(8,128)(2,1)S(1)} %get-tuple-element.96), channel_id=1, source_target_pairs={{0,1},{1,2},{2,3},{4,5},{5,6},{6,7},{8,9},{9,10},{10,11},{12,13},{... | collective-permute-start | bytes 442376 | tf_op jit(solution)/shard_map/ppermute | solution.py:20
  50.9 1.3 collective-permute-start.5
  52.4 1.1 collective-permute-done.4
  53.5 4.4 %collective-permute-done.5 = bf16[6,1,32,384]{3,2,1,0:T(8,128)(2,1)S(1)} collective-permute-done((bf16[6,1,32,384]{3,2,1,0:T(8,128)(2,1)S(1)}, bf16[6,1,32,384]{3,2,1,0:T(8,128)(2,1)S(1)}, u32[]{:S(2)}, u32[]{:S(2)}) %collective-permute-start.5) | collective-permute-done | bytes 147488 | tf_op jit(solution)/shard_map/ppermute | solution.py:22
  58.0 0.7 slice.406
  58.8 0.6 fusion.127
  59.4 0.6 iota_compare_fusion.5
  60.0 17.7 %all-gather.9.cloned.1.call-done = bf16[64,2,32,384]{3,2,1,0:T(8,128)(2,1)} async-done(((bf16[2,2,32,384]{3,2,1,0:T(8,128)(2,1)}), bf16[64,2,32,384]{3,2,1,0:T(8,128)(2,1)}) %all-gather.9.cloned.1.call-update) | async-done | bytes 3145744 | tf_op jit(solution)/shard_map/all_gather | solution.py:121
  77.7 2.5 %select_reduce_fusion.1 = bf16[2,2,32,384]{3,2,1,0:T(8,128)(2,1)S(1)} fusion(bf16[32,2,2,32,384]{4,3,2,1,0:T(8,128)(2,1)} %bitcast.109, pred[32]{0:T(512)(128)(4,1)S(1)} %iota_compare_fusion.5), kind=kLoop, calls=%fused_computation.20 | loop fusion | flops 3096576 | bytes 3244064 | tf_op jit(solution)/shard_map/reduce_sum | solution.py:101
  80.3 3.4 %collective-permute-start = (bf16[6,1,32,384]{3,2,1,0:T(8,128)(2,1)S(1)}, bf16[6,1,32,384]{3,2,1,0:T(8,128)(2,1)S(1)}, u32[]{:S(2)}, u32[]{:S(2)}) collective-permute-start(bf16[6,1,32,384]{3,2,1,0:T(8,128)(2,1)S(1)} %get-tuple-element.101), channel_id=1, source_target_pairs={{0,1},{1,2},{2,3},{4,5},{5,6},{6,7},{8,9},{9,10},{10,11},{12,13},{... | collective-permute-start | bytes 442376 | tf_op jit(solution)/shard_map/ppermute | solution.py:20
  83.7 1.5 collective-permute-start.1
  85.2 0.6 iota_compare_fusion.4
  85.8 1.4 collective-permute-done
  87.2 4.1 %collective-permute-done.1 = bf16[6,1,32,384]{3,2,1,0:T(8,128)(2,1)S(1)} collective-permute-done((bf16[6,1,32,384]{3,2,1,0:T(8,128)(2,1)S(1)}, bf16[6,1,32,384]{3,2,1,0:T(8,128)(2,1)S(1)}, u32[]{:S(2)}, u32[]{:S(2)}) %collective-permute-start.1) | collective-permute-done | bytes 147488 | tf_op jit(solution)/shard_map/ppermute | solution.py:22
  92.3 6.9 %select_reduce_fusion.2 = (f32[4,384]{1,0:T(4,128)S(1)}, f32[4,2,8,5,384]{4,2,3,1,0:T(8,128)S(1)}) fusion(pred[8,5]{0,1:T(8,128)(4,1)S(1)} %copy-done.2, bf16[2,3,3,3,384,384]{5,4,3,2,1,0:T(8,128)(2,1)} %param.20, bf16[6,4,1,7,2,384]{5,3,4,1,0,2:T(8,128)(2,1)S(1)} %slice.315, bf16[6,4,1,8,5,384]{5,3,4,1,0,2:T(8,128)(2,1)S(1)} %copy.48), kind=kOutput, calls=%fused_computation.72 | convolution fusion | flops 2551749120 | bytes 9455656 | tf_op jit(solution)/shard_map/conv_general_dilated | solution.py:66
  99.4 9.2 %psum.58 = f32[4,32]{1,0:T(4,128)S(1)} all-reduce(f32[4,32]{1,0:T(4,128)S(1)} %reduce_sum.192), channel_id=1, replica_groups=mesh['stretch'=32,'space'=4] {'space'}, use_global_device_ids=true, to_apply=%region_9.10 | all-reduce | flops 128 | bytes 1024 | tf_op jit(solution)/shard_map/psum | solution.py:41
  109.5 8.3 %psum.59 = f32[4,32]{1,0:T(4,128)S(1)} all-reduce(f32[4,32]{1,0:T(4,128)S(1)} %reduce_sum.194), channel_id=1, replica_groups=mesh['stretch'=32,'space'=4] {'space'}, use_global_device_ids=true, to_apply=%region_12.13 | all-reduce | flops 128 | bytes 1024 | tf_op jit(solution)/shard_map/psum | solution.py:43
  118.0 7.0 %all-gather.13.cloned.1.call-done = bf16[64,2,32,384]{3,2,1,0:T(8,128)(2,1)} async-done(((bf16[2,2,32,384]{3,2,1,0:T(8,128)(2,1)}), bf16[64,2,32,384]{3,2,1,0:T(8,128)(2,1)}) %all-gather.13.cloned.1.call-update) | async-done | bytes 3145744 | tf_op jit(solution)/shard_map/all_gather | solution.py:134
  125.0 2.7 %fusion.13 = f32[2,2,32,384]{3,2,1,0:T(8,128)S(1)} fusion(bf16[32,2,2,32,384]{4,3,2,1,0:T(8,128)(2,1)} %bitcast.107, pred[32]{0:T(512)(128)(4,1)S(1)} %iota_compare_fusion.4), kind=kLoop, calls=%fused_computation.15 | loop fusion | flops 4669440 | bytes 3342368 | tf_op jit(solution)/shard_map/reduce_sum | solution.py:101
  128.5 10.5 %all-reduce.5 = (f32[4,32]{1,0:T(4,128)S(1)}, f32[4,32]{1,0:T(4,128)S(1)}) all-reduce(f32[4,32]{1,0:T(4,128)S(1)} %reduce_sum.200, f32[4,32]{1,0:T(4,128)S(1)} %reduce_sum.198), channel_id=1, replica_groups=mesh['stretch'=32,'space'=4] {'space'}, use_global_device_ids=true, to_apply=%region_20.21 | all-reduce | flops 256 | bytes 2048 | tf_op jit(solution)/shard_map/psum | solution.py:55
  139.4 0.7 slice.317
  141.3 12.9 %fusion.31 = f32[6,4,8,5,384]{4,2,3,1,0:T(8,128)S(1)} fusion(bf16[2,3,3,3,384,384]{5,4,3,2,1,0:T(8,128)(2,1)} %param.20, bf16[8,6,1,7,2,384]{5,3,4,1,0,2:T(8,128)(2,1)S(1)} %slice.332, bf16[8,6,1,8,5,384]{5,3,4,1,0,2:T(8,128)(2,1)S(1)} %copy.62, pred[8,5]{0,1:T(8,128)(4,1)S(1)} %copy-done.2), kind=kOutput, calls=%fused_computation.38 | convolution fusion | flops 7650680832 | bytes 11427880 | tf_op jit(solution)/shard_map/conv_general_dilated | solution.py:79
  155.0 1.5 collective-permute-start.6
  156.5 1.3 collective-permute-start.7
  158.0 1.1 collective-permute-done.6
  159.2 4.4 %collective-permute-done.7 = bf16[6,1,32,384]{3,2,1,0:T(8,128)(2,1)S(1)} collective-permute-done((bf16[6,1,32,384]{3,2,1,0:T(8,128)(2,1)S(1)}, bf16[6,1,32,384]{3,2,1,0:T(8,128)(2,1)S(1)}, u32[]{:S(2)}, u32[]{:S(2)}) %collective-permute-start.7) | collective-permute-done | bytes 147488 | tf_op jit(solution)/shard_map/ppermute | solution.py:22
  163.7 0.6 slice.405
  164.3 18.2 %all-gather.11.cloned.1.call-done = bf16[64,2,32,384]{3,2,1,0:T(8,128)(2,1)} async-done(((bf16[2,2,32,384]{3,2,1,0:T(8,128)(2,1)}), bf16[64,2,32,384]{3,2,1,0:T(8,128)(2,1)}) %all-gather.11.cloned.1.call-update) | async-done | bytes 3145744 | tf_op jit(solution)/shard_map/all_gather | solution.py:121
  182.5 2.5 %select_reduce_fusion = bf16[2,2,32,384]{3,2,1,0:T(8,128)(2,1)S(1)} fusion(bf16[32,2,2,32,384]{4,3,2,1,0:T(8,128)(2,1)} %bitcast.108, pred[32]{0:T(512)(128)(4,1)S(1)} %iota_compare_fusion.5), kind=kLoop, calls=%fused_computation.19 | loop fusion | flops 3096576 | bytes 3244064 | tf_op jit(solution)/shard_map/reduce_sum | solution.py:101
  185.1 3.4 %collective-permute-start.2 = (bf16[6,1,32,384]{3,2,1,0:T(8,128)(2,1)S(1)}, bf16[6,1,32,384]{3,2,1,0:T(8,128)(2,1)S(1)}, u32[]{:S(2)}, u32[]{:S(2)}) collective-permute-start(bf16[6,1,32,384]{3,2,1,0:T(8,128)(2,1)S(1)} %get-tuple-element.99), channel_id=1, source_target_pairs={{0,1},{1,2},{2,3},{4,5},{5,6},{6,7},{8,9},{9,10},{10,11},{12,13},{... | collective-permute-start | bytes 442376 | tf_op jit(solution)/shard_map/ppermute | solution.py:20
  188.5 1.6 collective-permute-start.3
  190.1 1.9 collective-permute-done.2
  192.0 4.1 %collective-permute-done.3 = bf16[6,1,32,384]{3,2,1,0:T(8,128)(2,1)S(1)} collective-permute-done((bf16[6,1,32,384]{3,2,1,0:T(8,128)(2,1)S(1)}, bf16[6,1,32,384]{3,2,1,0:T(8,128)(2,1)S(1)}, u32[]{:S(2)}, u32[]{:S(2)}) %collective-permute-start.3) | collective-permute-done | bytes 147488 | tf_op jit(solution)/shard_map/ppermute | solution.py:22
  197.1 6.9 %fusion.47 = bf16[4,2,8,5,384]{4,2,3,1,0:T(8,128)(2,1)S(1)} fusion(bf16[2,3,3,3,384,384]{5,4,3,2,1,0:T(8,128)(2,1)} %param.20, bf16[6,4,1,7,2,384]{5,3,4,1,0,2:T(8,128)(2,1)S(1)} %slice.320, bf16[6,4,1,8,5,384]{5,3,4,1,0,2:T(8,128)(2,1)S(1)} %copy.53, pred[8,5]{0,1:T(8,128)(4,1)S(1)} %copy-done.2), kind=kOutput, calls=%fused_computation.43 | convolution fusion | flops 2551382016 | bytes 9203752 | tf_op jit(solution)/shard_map/conv_general_dilated | solution.py:66
  204.4 0.7 copy.65
  205.1 24.0 %all-gather.15.cloned.1.call-done = bf16[64,2,32,384]{3,2,1,0:T(8,128)(2,1)} async-done(((bf16[2,2,32,384]{3,2,1,0:T(8,128)(2,1)}), bf16[64,2,32,384]{3,2,1,0:T(8,128)(2,1)}) %all-gather.15.cloned.1.call-update) | async-done | bytes 3145744 | tf_op jit(solution)/shard_map/all_gather | solution.py:134
  229.1 2.7 %fusion.12 = f32[2,2,32,384]{3,2,1,0:T(8,128)S(1)} fusion(bf16[32,2,2,32,384]{4,3,2,1,0:T(8,128)(2,1)} %bitcast.110, pred[32]{0:T(512)(128)(4,1)S(1)} %iota_compare_fusion.4), kind=kLoop, calls=%fused_computation.13 | loop fusion | flops 4669440 | bytes 3342368 | tf_op jit(solution)/shard_map/reduce_sum | solution.py:101
  232.6 10.5 %all-reduce.4 = (f32[4,32]{1,0:T(4,128)S(1)}, f32[4,32]{1,0:T(4,128)S(1)}) all-reduce(f32[4,32]{1,0:T(4,128)S(1)} %reduce_sum.205, f32[4,32]{1,0:T(4,128)S(1)} %reduce_sum.203), channel_id=1, replica_groups=mesh['stretch'=32,'space'=4] {'space'}, use_global_device_ids=true, to_apply=%region_27.28 | all-reduce | flops 256 | bytes 2048 | tf_op jit(solution)/shard_map/psum | solution.py:55
  243.4 0.8 fusion.96
  (103 shorter events, 11.0 us)
Async XLA Ops:
  7.2 70.5 %all-gather.9.cloned.1.call-start = ((), (), s32[]{:S(2)}) async-start(), calls=%async_computation | async-start | bytes 3244032 | tf_op jit(solution)/shard_map/all_gather | solution.py:121
  31.2 93.9 %all-gather.13.cloned.1.call-start = ((), (), s32[]{:S(2)}) async-start(), calls=%async_computation.2 | async-start | bytes 3244032 | tf_op jit(solution)/shard_map/all_gather | solution.py:134
  32.6 0.7 copy-start.2
  46.9 6.6 %collective-permute-start.4 = (bf16[6,1,32,384]{3,2,1,0:T(8,128)(2,1)S(1)}, bf16[6,1,32,384]{3,2,1,0:T(8,128)(2,1)S(1)}, u32[]{:S(2)}, u32[]{:S(2)}) collective-permute-start(bf16[6,1,32,384]{3,2,1,0:T(8,128)(2,1)S(1)} %get-tuple-element.96), channel_id=1, source_target_pairs={{0,1},{1,2},{2,3},{4,5},{5,6},{6,7},{8,9},{9,10},{10,11},{12,13},{... | collective-permute-start | bytes 442376 | tf_op jit(solution)/shard_map/ppermute | solution.py:20
  50.9 7.0 %collective-permute-start.5 = (bf16[6,1,32,384]{3,2,1,0:T(8,128)(2,1)S(1)}, bf16[6,1,32,384]{3,2,1,0:T(8,128)(2,1)S(1)}, u32[]{:S(2)}, u32[]{:S(2)}) collective-permute-start(bf16[6,1,32,384]{3,2,1,0:T(8,128)(2,1)S(1)} %get-tuple-element.97), channel_id=1, source_target_pairs={{1,0},{2,1},{3,2},{5,4},{6,5},{7,6},{9,8},{10,9},{11,10},{13,12},{... | collective-permute-start | bytes 442376 | tf_op jit(solution)/shard_map/ppermute | solution.py:22
  52.3 6.4 %copy-start.1 = (s32[1,4]{1,0:T(1,128)S(1)}, s32[1,4]{1,0:T(1,128)}, u32[]{:S(2)}) copy-start(s32[1,4]{1,0:T(1,128)} %param.19) | copy-start | bytes 52
  58.7 123.8 %all-gather.11.cloned.1.call-start = ((), (), s32[]{:S(2)}) async-start(), calls=%async_computation.1 | async-start | bytes 3244032 | tf_op jit(solution)/shard_map/all_gather | solution.py:121
  80.3 6.9 %collective-permute-start = (bf16[6,1,32,384]{3,2,1,0:T(8,128)(2,1)S(1)}, bf16[6,1,32,384]{3,2,1,0:T(8,128)(2,1)S(1)}, u32[]{:S(2)}, u32[]{:S(2)}) collective-permute-start(bf16[6,1,32,384]{3,2,1,0:T(8,128)(2,1)S(1)} %get-tuple-element.101), channel_id=1, source_target_pairs={{0,1},{1,2},{2,3},{4,5},{5,6},{6,7},{8,9},{9,10},{10,11},{12,13},{... | collective-permute-start | bytes 442376 | tf_op jit(solution)/shard_map/ppermute | solution.py:20
  83.7 7.6 %collective-permute-start.1 = (bf16[6,1,32,384]{3,2,1,0:T(8,128)(2,1)S(1)}, bf16[6,1,32,384]{3,2,1,0:T(8,128)(2,1)S(1)}, u32[]{:S(2)}, u32[]{:S(2)}) collective-permute-start(bf16[6,1,32,384]{3,2,1,0:T(8,128)(2,1)S(1)} %get-tuple-element.102), channel_id=1, source_target_pairs={{1,0},{2,1},{3,2},{5,4},{6,5},{7,6},{9,8},{10,9},{11,10},{13,12},{... | collective-permute-start | bytes 442376 | tf_op jit(solution)/shard_map/ppermute | solution.py:22
  140.0 89.1 %all-gather.15.cloned.1.call-start = ((), (), s32[]{:S(2)}) async-start(), calls=%async_computation.3 | async-start | bytes 3244032 | tf_op jit(solution)/shard_map/all_gather | solution.py:134
  155.0 4.2 %collective-permute-start.6 = (bf16[6,1,32,384]{3,2,1,0:T(8,128)(2,1)S(1)}, bf16[6,1,32,384]{3,2,1,0:T(8,128)(2,1)S(1)}, u32[]{:S(2)}, u32[]{:S(2)}) collective-permute-start(bf16[6,1,32,384]{3,2,1,0:T(8,128)(2,1)S(1)} %get-tuple-element.94), channel_id=1, source_target_pairs={{0,1},{1,2},{2,3},{4,5},{5,6},{6,7},{8,9},{9,10},{10,11},{12,13},{... | collective-permute-start | bytes 442376 | tf_op jit(solution)/shard_map/ppermute | solution.py:20
  156.5 7.0 %collective-permute-start.7 = (bf16[6,1,32,384]{3,2,1,0:T(8,128)(2,1)S(1)}, bf16[6,1,32,384]{3,2,1,0:T(8,128)(2,1)S(1)}, u32[]{:S(2)}, u32[]{:S(2)}) collective-permute-start(bf16[6,1,32,384]{3,2,1,0:T(8,128)(2,1)S(1)} %get-tuple-element.95), channel_id=1, source_target_pairs={{1,0},{2,1},{3,2},{5,4},{6,5},{7,6},{9,8},{10,9},{11,10},{13,12},{... | collective-permute-start | bytes 442376 | tf_op jit(solution)/shard_map/ppermute | solution.py:22
  185.1 6.9 %collective-permute-start.2 = (bf16[6,1,32,384]{3,2,1,0:T(8,128)(2,1)S(1)}, bf16[6,1,32,384]{3,2,1,0:T(8,128)(2,1)S(1)}, u32[]{:S(2)}, u32[]{:S(2)}) collective-permute-start(bf16[6,1,32,384]{3,2,1,0:T(8,128)(2,1)S(1)} %get-tuple-element.99), channel_id=1, source_target_pairs={{0,1},{1,2},{2,3},{4,5},{5,6},{6,7},{8,9},{9,10},{10,11},{12,13},{... | collective-permute-start | bytes 442376 | tf_op jit(solution)/shard_map/ppermute | solution.py:20
  188.5 7.6 %collective-permute-start.3 = (bf16[6,1,32,384]{3,2,1,0:T(8,128)(2,1)S(1)}, bf16[6,1,32,384]{3,2,1,0:T(8,128)(2,1)S(1)}, u32[]{:S(2)}, u32[]{:S(2)}) collective-permute-start(bf16[6,1,32,384]{3,2,1,0:T(8,128)(2,1)S(1)} %get-tuple-element.100), channel_id=1, source_target_pairs={{1,0},{2,1},{3,2},{5,4},{6,5},{7,6},{9,8},{10,9},{11,10},{13,12},{... | collective-permute-start | bytes 442376 | tf_op jit(solution)/shard_map/ppermute | solution.py:22
  205.1 26.7 %copy-start = (bf16[4,2,32,384]{3,2,1,0:T(8,128)(2,1)S(1)}, bf16[4,2,32,384]{3,2,1,0:T(8,128)(2,1)}, u32[]{:S(2)}) copy-start(bf16[4,2,32,384]{3,2,1,0:T(8,128)(2,1)} %param.18) | copy-start | bytes 589828
Sparse Core Ops, SparseCore 0:
  31.3 46.3 all-gather.8
  80.5 44.4 all-gather.12
  140.2 42.2 all-gather.10
  184.6 44.4 all-gather.14
where the time goes:
time: 252 us; the launch traced here: 251 us
  waiting for transfers between devices  89.5 us (36%)
  blocking collectives  57.1 us (23%)
  matrix products  39.6 us (16%)
  starting transfers between devices  18.2 us (7%)
  other arithmetic  18 us (7%)
  between operations  14.4 us (6%)
  local copies, waits for them, and re-layouts  14 us (6%)
    all_gather x2, waiting for transfers between devices, per_device(): lax.all_gather(activated[FRAMES - 2:][None], 'stretch', axis=0, tiled=True)  35.8 us
    all_gather x2, waiting for transfers between devices, per_device(): lax.all_gather(a, 'stretch', axis=0, tiled=True)  31 us
    conv_general_dilated x2, matrix products, conv_adjoint(): lax.conv_general_dilated(padded[None], flipped, (1, 1, 1), 'VALID', dimen...  25.8 us
    psum x2, blocking collectives, norm_backward(): lax.psum((group_totals(grad_normed), group_totals(grad_normed * normed)),...  21 us
    psum x2, blocking collectives, norm_forward(): mean_val = lax.psum(group_totals(acts_f32), 'space') / cell_count  20.1 us
    ppermute x4, waiting for transfers between devices, with_halo(): lax.ppermute(head, axis, [((i + 1) % count, i) for i in range(ends)])  17 us
    psum x2, blocking collectives, norm_forward(): variance = lax.psum(group_totals(centered * centered), 'space') / cell_count  16.1 us
    conv_general_dilated x2, matrix products, conv_forward(): lax.conv_general_dilated(padded[None], kernel, (1, 1, 1), 'VALID', dimens...  13.8 us
  transfers between devices with their start and end apart: 12, of which 12 were waited for; matrix products, arithmetic and copies ran while one was open for 23% of the time, Pallas kernels for 0%

commit v1 on v0

v1 whole, which is shorter than its diff:
```python
import jax
import jax.numpy as jnp
from jax import lax
from jax.experimental import pallas as pl
from jax.experimental.pallas import tpu as pltpu
from jax.sharding import PartitionSpec as P

C = 384
GROUPS = 32
GSIZE = C // GROUPS
COLS = 32
ROWS = 8
CELLS = ROWS * COLS
PADDED = CELLS + 2 * COLS
COUNT = float(CELLS * GSIZE)
F32 = jnp.float32
BF16 = jnp.bfloat16
VMEM = pl.BlockSpec(memory_space=pltpu.VMEM)
SMEM = pl.BlockSpec(memory_space=pltpu.SMEM)
ANY = pl.BlockSpec(memory_space=pl.ANY)


def group_matrix():
    row = lax.broadcasted_iota(jnp.int32, (C, C), 0) // GSIZE
    col = lax.broadcasted_iota(jnp.int32, (C, C), 1) // GSIZE
    return (row == col).astype(BF16)


def group_mean(sums, ones):
    n = sums.shape[0]
    high = sums.astype(BF16)
    rest = sums - high.astype(F32)
    mid = rest.astype(BF16)
    low = (rest - mid.astype(F32)).astype(BF16)
    parts = jnp.dot(
        jnp.concatenate([high.astype(F32), mid.astype(F32), low.astype(F32)], axis=0).astype(BF16),
        ones[...],
        preferred_element_type=F32,
    )
    return (parts[:n] + parts[n : 2 * n] + parts[2 * n :]) * (1.0 / COUNT)


def fold(values):
    return jnp.sum(values.reshape(COLS // 8, 8, C), axis=0)


def sigmoid(v):
    return 0.5 * jnp.tanh(0.5 * v) + 0.5


def store_shifted(slab, idx, row, values):
    col = lax.broadcasted_iota(jnp.int32, (COLS, C), 0)
    left = jnp.where(col == 0, 0.0, pltpu.roll(values, 1, 0))
    right = jnp.where(col == COLS - 1, 0.0, pltpu.roll(values, COLS - 1, 0))
    at = pl.ds(row * COLS, COLS)
    slab[idx, at, 0:C] = left.astype(BF16)
    slab[idx, at, C : 2 * C] = values.astype(BF16)
    slab[idx, at, 2 * C : 3 * C] = right.astype(BF16)


def conv_tap(slab_in, taps, a, acc, f):
    w = jnp.concatenate(
        [taps[pl.ds(a * 9 + 3 * b, 3)].reshape(3 * C, C) for b in range(3)], axis=1
    )
    y = jnp.dot(slab_in, w, preferred_element_type=F32)
    for b in range(3):
        acc[f, (2 - b) * COLS : (2 - b) * COLS + CELLS, :] += y[:, b * C : (b + 1) * C]


def adjoint_tap(slab_in, taps, a, acc, f):
    w = jnp.concatenate(
        [
            jnp.concatenate([taps[a * 9 + 3 * b + 2 - e] for e in range(3)], axis=1)
            for b in range(3)
        ],
        axis=0,
    )
    y = lax.dot_general(slab_in, w, (((1,), (1,)), ((), ())), preferred_element_type=F32)
    for b in range(3):
        acc[f, b * COLS : b * COLS + CELLS, :] += y[:, b * C : (b + 1) * C]


def frame_sums(x, idx):
    def body(r, tot):
        return tot + fold(x[idx, pl.ds(r * COLS, COLS), :].astype(F32))

    tot = lax.fori_loop(0, ROWS, body, jnp.zeros((8, C), F32), unroll=True)
    return jnp.sum(tot, axis=0, keepdims=True)


def frame_square_sums(x, idx, mean):
    def body(r, tot):
        diff = x[idx, pl.ds(r * COLS, COLS), :].astype(F32) - mean
        return tot + fold(diff * diff)

    tot = lax.fori_loop(0, ROWS, body, jnp.zeros((8, C), F32), unroll=True)
    return jnp.sum(tot, axis=0, keepdims=True)


def frame_stats(x, count, sums, mean, inv_std, ones):
    sums[...] = jnp.zeros_like(sums)

    def total(n, _):
        sums[pl.ds(n, 1), :] = frame_sums(x, n)
        return 0

    lax.fori_loop(0, count, total, 0)
    mean[...] = group_mean(sums[...], ones)

    def square(n, _):
        sums[pl.ds(n, 1), :] = frame_square_sums(x, n, mean[pl.ds(n, 1), :])
        return 0

    lax.fori_loop(0, count, square, 0)
    inv_std[...] = lax.rsqrt(group_mean(sums[...], ones) + 1e-5)


def norm_silu_frame(x, idx, mean, inv_std, gain, bias, slab, out_idx, mask):
    scale = inv_std * gain

    def body(r, _):
        v = (x[idx, pl.ds(r * COLS, COLS), :].astype(F32) - mean) * scale + bias
        s = v * sigmoid(v)
        if mask is not None:
            s = s * mask
        store_shifted(slab, out_idx, r, s)
        return 0

    lax.fori_loop(0, ROWS, body, 0, unroll=2)


def norm_back_sums(x, idx, mean, inv_std, gain, bias, acc, f):
    def body(r, tot):
        at = pl.ds(COLS + r * COLS, COLS)
        n = (x[idx, pl.ds(r * COLS, COLS), :].astype(F32) - mean) * inv_std
        v = n * gain + bias
        sig = sigmoid(v)
        gn = acc[f, at, :] * (sig * (1.0 + v * (1.0 - sig)) * gain)
        acc[f, at, :] = gn
        return tot[0] + fold(gn), tot[1] + fold(gn * n)

    zero = jnp.zeros((8, C), F32)
    one, two = lax.fori_loop(0, ROWS, body, (zero, zero), unroll=2)
    return jnp.sum(one, axis=0, keepdims=True), jnp.sum(two, axis=0, keepdims=True)


def norm_back_row(x, idx, r, mean, inv_std, acc, f, first, second):
    n = (x[idx, pl.ds(r * COLS, COLS), :].astype(F32) - mean) * inv_std
    return inv_std * (acc[f, pl.ds(COLS + r * COLS, COLS), :] - first - n * second)


def read_row(block):
    parts = [block(cb).astype(F32) for cb in range(4)]
    raw = jnp.concatenate([p[:8] for p in parts], axis=0)
    cot = jnp.concatenate([p[8:] for p in parts], axis=0)
    return raw, cot


def start_weights(weight, taps, sems):
    for layer in range(2):
        for a in range(3):
            pltpu.make_async_copy(
                weight.at[layer, pl.ds(a * 9, 9)],
                taps.at[layer, pl.ds(a * 9, 9)],
                sems.at[layer, a],
            ).start()


def wait_weights(weight, taps, sems, layer):
    for a in range(3):
        pltpu.make_async_copy(
            weight.at[layer, pl.ds(a * 9, 9)], taps.at[layer, pl.ds(a * 9, 9)], sems.at[layer, a]
        ).wait()


def route_kernel(place, table, pieces, out):
    g = place[0] // 8

    def body(d, _):
        nxt, prv = table[d, 2], table[d, 3]
        for j in range(4):
            src = jnp.where(j <= g, prv, jnp.where(j >= g + 2, nxt, -1))
            cot_src = jnp.where(j >= g, nxt, -1)
            raw = pieces[jnp.maximum(src, 0)].astype(F32)[:8]
            cot = pieces[jnp.maximum(cot_src, 0)].astype(F32)[8:]
            raw = raw * (src >= 0).astype(F32)
            cot = cot * (cot_src >= 0).astype(F32)
            out[d * 4 + j] = jnp.concatenate([raw, cot], axis=0).astype(BF16)
        return 0

    lax.fori_loop(0, 32, body, 0)


def own_kernel(
    place, mine, from1, from2, from3, gain, bias, weight, acc0, acc1,
    taps, x, slab, gslab, sums, mean, inv_std, ones, sems,
):
    start_weights(weight, taps, sems)
    j = place[1]
    ones[...] = group_matrix()
    acc0[...] = jnp.zeros_like(acc0)
    acc1[...] = jnp.zeros_like(acc1)
    for shift, part in enumerate((mine, from1, from2, from3)):
        holder = lax.rem(j + 4 - shift, 4)

        def rows(t, _, part=part, holder=holder):
            g, r = t // 2, lax.rem(t, 2)
            raw, cot = read_row(lambda cb: part[t * 4 + cb])
            x[g, pl.ds((holder * 2 + r) * COLS, COLS), :] = raw.astype(BF16)
            store_shifted(gslab, g, holder * 2 + r, cot)
            return 0

        lax.fori_loop(0, 8, rows, 0)
    frame_stats(x, 4, sums, mean, inv_std, ones)

    def normed(g, _):
        norm_silu_frame(
            x, g, mean[pl.ds(g, 1), :], inv_std[pl.ds(g, 1), :],
            gain[0:1, :], bias[0:1, :], slab, g, None,
        )
        return 0

    lax.fori_loop(0, 4, normed, 0)
    wait_weights(weight, taps, sems, 0)

    def forward(t, _):
        g, a = t // 3, lax.rem(t, 3)
        f = g + 4 - j - a

        @pl.when((f >= 0) & (f <= 4))
        def _():
            conv_tap(slab[g], taps.at[0], a, acc0, f)

        return 0

    lax.fori_loop(0, 12, forward, 0)
    wait_weights(weight, taps, sems, 1)

    def backward(t, _):
        g, a = t // 3, lax.rem(t, 3)
        u = g - j
        f = u - 2 + a

        @pl.when((u >= 0) & (f >= 0) & (f <= 2))
        def _():
            adjoint_tap(gslab[g], taps.at[1], a, acc1, f)

        return 0

    lax.fori_loop(0, 12, backward, 0)


def rest_kernel(
    place, mine, from1, from2, from3, recv, acc0_in, acc1_in, gain, bias, weight, out,
    taps, x, slab, gslab, acc0, acc1, acc2, h, sums, mean, inv_std, ones, raw_own, sems,
):
    start_weights(weight, taps, sems)
    j = place[1]
    has_prev = (place[2] >= 0).astype(F32)
    ones[...] = group_matrix()
    acc0[...] = acc0_in[...]
    acc1[...] = acc1_in[...]

    for shift, part in enumerate((mine, from1, from2, from3)):
        holder = lax.rem(j + 4 - shift, 4)
        for r in range(2):
            raw, _ = read_row(lambda cb: part[(j * 2 + r) * 4 + cb])
            raw_own[0, pl.ds((holder * 2 + r) * COLS, COLS), :] = raw.astype(BF16)

    def rows(t, _):
        g, row = t // 8, lax.rem(t, 8)
        i, r = row // 2, lax.rem(row, 2)
        raw, cot = read_row(lambda cb: recv[((g * 2 + r) * 4 + cb) * 4 + i])
        x[g, pl.ds(row * COLS, COLS), :] = raw.astype(BF16)
        store_shifted(gslab, g, row, cot)
        return 0

    lax.fori_loop(0, 32, rows, 0)
    frame_stats(x, 4, sums, mean, inv_std, ones)

    def normed(g, _):
        mask = jnp.where(g >= j, has_prev, 1.0)
        norm_silu_frame(
            x, g, mean[pl.ds(g, 1), :], inv_std[pl.ds(g, 1), :],
            gain[0:1, :], bias[0:1, :], slab, g, mask,
        )
        return 0

    lax.fori_loop(0, 4, normed, 0)
    wait_weights(weight, taps, sems, 0)

    def forward(t, _):
        g, a = t // 3, lax.rem(t, 3)
        w = jnp.where(g >= j, g - j, g - j + 8)
        f = w - a

        @pl.when((f >= 0) & (f <= 4) & (g != j - 1))
        def _():
            conv_tap(slab[g], taps.at[0], a, acc0, f)

        return 0

    lax.fori_loop(0, 12, forward, 0)
    wait_weights(weight, taps, sems, 1)

    def backward(t, _):
        g, a = t // 3, lax.rem(t, 3)
        u = g + 4 - j
        f = u - 2 + a

        @pl.when((u <= 4) & (f >= 0) & (f <= 2))
        def _():
            adjoint_tap(gslab[g], taps.at[1], a, acc1, f)

        return 0

    lax.fori_loop(0, 12, backward, 0)

    def rounded(f, _):
        h[f] = acc0[f, COLS : COLS + CELLS, :].astype(BF16)
        return 0

    lax.fori_loop(0, 5, rounded, 0)
    frame_stats(h, 5, sums, mean, inv_std, ones)
    gain1, bias1 = gain[1:2, :], bias[1:2, :]

    def normed1(f, _):
        mask = jnp.where(j - 2 + f < 0, has_prev, 1.0)
        norm_silu_frame(
            h, f, mean[pl.ds(f, 1), :], inv_std[pl.ds(f, 1), :], gain1, bias1, slab, f, mask
        )
        return 0

    lax.fori_loop(0, 3, normed1, 0)
    acc2[...] = jnp.zeros_like(acc2)

    def last(a, _):
        conv_tap(slab[a], taps.at[1], a, acc2, 0)
        return 0

    lax.fori_loop(0, 3, last, 0)
    for i in range(4):
        out[i, 0] = acc2[0, COLS + i * 64 : COLS + i * 64 + 64, :].astype(BF16)

    sums[...] = jnp.zeros_like(sums)

    def back_sums(f, _):
        n = f + 2
        one, two = norm_back_sums(
            h, n, mean[pl.ds(n, 1), :], inv_std[pl.ds(n, 1), :], gain1, bias1, acc1, f
        )
        sums[pl.ds(f, 1), :] = one
        sums[pl.ds(f + 4, 1), :] = two
        return 0

    lax.fori_loop(0, 3, back_sums, 0)
    sums[...] = group_mean(sums[...], ones)

    def back_rows(t, _):
        f, r = t // 8, lax.rem(t, 8)
        n = f + 2
        g1 = norm_back_row(
            h, n, r, mean[pl.ds(n, 1), :], inv_std[pl.ds(n, 1), :], acc1, f,
            sums[pl.ds(f, 1), :], sums[pl.ds(f + 4, 1), :],
        )
        store_shifted(slab, f, r, g1)
        return 0

    lax.fori_loop(0, 24, back_rows, 0)
    acc2[...] = jnp.zeros_like(acc2)

    def first(a, _):
        adjoint_tap(slab[2 - a], taps.at[0], a, acc2, 0)
        return 0

    lax.fori_loop(0, 3, first, 0)

    frame_stats(raw_own, 1, sums, mean, inv_std, ones)
    m0, i0 = mean[0:1, :], inv_std[0:1, :]
    one, two = norm_back_sums(raw_own, 0, m0, i0, gain[0:1, :], bias[0:1, :], acc2, 0)
    sums[0:1, :] = one
    sums[1:2, :] = two
    sums[...] = group_mean(sums[...], ones)
    for r in range(8):
        g0 = norm_back_row(raw_own, 0, r, m0, i0, acc2, 0, sums[0:1, :], sums[1:2, :])
        out[r // 2, 1, (r % 2) * COLS : (r % 2 + 1) * COLS, :] = g0.astype(BF16)


def per_device(frames, stretch_table, conv_weight, norm_gain, norm_bias, cotangent):
    params = pltpu.CompilerParams(vmem_limit_bytes=58 * 2**20)
    stretch, space = lax.axis_index("stretch"), lax.axis_index("space")
    place = jnp.stack([stretch, space, stretch_table[0, 3], stretch_table[0, 2]]).astype(jnp.int32)
    pieces = jnp.concatenate([frames.reshape(32, 8, C), cotangent.reshape(32, 8, C)], axis=1)
    weight = conv_weight.reshape(2, 27, C, C)
    table = lax.all_gather(stretch_table, "stretch", axis=0, tiled=True)
    spread = lax.all_to_all(pieces, "stretch", 0, 0, tiled=True)
    shifted = [
        lax.ppermute(pieces, "space", [(i, (i + k) % 4) for i in range(4)]) for k in (1, 2, 3)
    ]
    routed = pl.pallas_call(
        route_kernel,
        out_shape=jax.ShapeDtypeStruct((128, 16, C), BF16),
        in_specs=[SMEM, SMEM, VMEM],
        out_specs=VMEM,
        name="route",
    )(place, table, spread)
    recv = lax.all_to_all(routed, ("stretch", "space"), 0, 0, tiled=True)
    acc0, acc1 = pl.pallas_call(
        own_kernel,
        out_shape=[
            jax.ShapeDtypeStruct((5, PADDED, C), F32),
            jax.ShapeDtypeStruct((3, PADDED, C), F32),
        ],
        in_specs=[SMEM, VMEM, VMEM, VMEM, VMEM, VMEM, VMEM, ANY],
        out_specs=[VMEM, VMEM],
        scratch_shapes=[
            pltpu.VMEM((2, 27, C, C), BF16),
            pltpu.VMEM((4, CELLS, C), BF16),
            pltpu.VMEM((4, CELLS, 3 * C), BF16),
            pltpu.VMEM((4, CELLS, 3 * C), BF16),
            pltpu.VMEM((8, C), F32),
            pltpu.VMEM((8, C), F32),
            pltpu.VMEM((8, C), F32),
            pltpu.VMEM((C, C), BF16),
            pltpu.SemaphoreType.DMA((2, 3)),
        ],
        compiler_params=params,
        cost_estimate=pl.CostEstimate(
            flops=15 * 2 * CELLS * 9 * C * C, bytes_accessed=24 * 2**20, transcendentals=0
        ),
        name="own",
    )(place, pieces, *shifted, norm_gain, norm_bias, weight)
    out = pl.pallas_call(
        rest_kernel,
        out_shape=jax.ShapeDtypeStruct((4, 2, 64, C), BF16),
        in_specs=[SMEM, VMEM, VMEM, VMEM, VMEM, VMEM, VMEM, VMEM, VMEM, VMEM, ANY],
        out_specs=VMEM,
        scratch_shapes=[
            pltpu.VMEM((2, 27, C, C), BF16),
            pltpu.VMEM((4, CELLS, C), BF16),
            pltpu.VMEM((4, CELLS, 3 * C), BF16),
            pltpu.VMEM((4, CELLS, 3 * C), BF16),
            pltpu.VMEM((5, PADDED, C), F32),
            pltpu.VMEM((3, PADDED, C), F32),
            pltpu.VMEM((1, PADDED, C), F32),
            pltpu.VMEM((5, CELLS, C), BF16),
            pltpu.VMEM((8, C), F32),
            pltpu.VMEM((8, C), F32),
            pltpu.VMEM((8, C), F32),
            pltpu.VMEM((C, C), BF16),
            pltpu.VMEM((1, CELLS, C), BF16),
            pltpu.SemaphoreType.DMA((2, 3)),
        ],
        compiler_params=params,
        cost_estimate=pl.CostEstimate(
            flops=18 * 2 * CELLS * 9 * C * C, bytes_accessed=24 * 2**20, transcendentals=0
        ),
        name="rest",
    )(place, pieces, *shifted, recv, acc0, acc1, norm_gain, norm_bias, weight)
    back = lax.all_to_all(out, "space", 0, 0, tiled=True)
    shape = frames.shape
    return back[:, 0].reshape(shape), back[:, 1].reshape(shape)


def solution(mesh):
    in_specs = (
        P("stretch", "space", None, None),
        P("stretch", None),
        P(),
        P(),
        P(),
        P("stretch", "space", None, None),
    )
    out_specs = (P("stretch", "space", None, None), P("stretch", "space", None, None))
    return jax.shard_map(
        per_device, mesh=mesh, in_specs=in_specs, out_specs=out_specs, check_vma=False
    )
```

time: 252 us -> 152 us (0.60)
  waiting for transfers between devices: 89.5 us -> 32.3 us
  Pallas kernels: 0 us -> 53.6 us
  matrix products: 39.6 us -> 0 us
  blocking collectives: 57.1 us -> 35.8 us
  other arithmetic: 18 us -> 3.77 us
  between operations: 14.4 us -> 0.71 us
  local copies, waits for them, and re-layouts: 14 us -> 3.99 us
  starting transfers between devices: 18.2 us -> 20.8 us
    all_gather x4 -> x0, waiting for transfers between devices: 66.8 us -> none  [the longest x2 35.8 us: per_device(): lax.all_gather(activated[FRAMES - 2:][None], 'stretch', axis=0, tiled=True)]
    psum x6 -> x0, blocking collectives: 57.1 us -> none  [the longest x2 21 us: norm_backward(): lax.psum((group_totals(grad_normed), group_totals(grad_normed * normed)),...]
    pallas_call x0 -> x3, Pallas kernels: none -> 53.6 us  [the longest x1 28.6 us: per_device(): pl.pallas_call(rest_kernel, out_shape=jax.ShapeDtypeStruct((4, 2, 64, C),...]
    conv_general_dilated x4 -> x0, matrix products: 39.6 us -> none  [the longest x2 25.8 us: conv_adjoint(): lax.conv_general_dilated(padded[None], flipped, (1, 1, 1), 'VALID', dimen...]
    all_gather x0 -> x1, blocking collectives: none -> 24.3 us  [per_device(): table = lax.all_gather(stretch_table, 'stretch', axis=0, tiled=True)]
    all_to_all x0 -> x2, starting transfers between devices: none -> 16.9 us  [the longest x1 8.63 us: per_device(): recv = lax.all_to_all(routed, ('stretch', 'space'), 0, 0, tiled=True)]
    ppermute x8 -> x3, starting transfers between devices: 17.9 us -> 3.96 us  [per_device(): lax.ppermute(pieces, 'space', [(i, (i + k) % 4) for i in range(4)])]
    reduce_sum x17 -> x0, other arithmetic: 13.8 us -> none  [the longest x4 10.5 us: chooser(): return running + jnp.sum(picked, axis=0).astype(running.dtype)]
  transfers between devices with their start and end apart: 12 -> 5, of which waited for: 12 -> 3; matrix products, arithmetic and copies ran while one was open for 23% -> 2% of each run, Pallas kernels for 0% -> 14%
where the time goes in v1:
time: 152 us; the launch traced here: 151 us
  Pallas kernels  53.6 us (35%)
  blocking collectives  35.8 us (24%)
  waiting for transfers between devices  32.3 us (21%)
  starting transfers between devices  20.8 us (14%)
  local copies, waits for them, and re-layouts  3.99 us (3%)
  other arithmetic  3.77 us (2%)
    ppermute x3, waiting for transfers between devices, per_device(): lax.ppermute(pieces, 'space', [(i, (i + k) % 4) for i in range(4)])  32.3 us
    pallas_call x1, Pallas kernels, per_device(): pl.pallas_call(rest_kernel, out_shape=jax.ShapeDtypeStruct((4, 2, 64, C),...  28.6 us
    all_gather x1, blocking collectives, per_device(): table = lax.all_gather(stretch_table, 'stretch', axis=0, tiled=True)  24.3 us
    pallas_call x1, Pallas kernels, per_device(): pl.pallas_call(own_kernel, out_shape=[jax.ShapeDtypeStruct((5, PADDED, C)...  21.7 us
    all_to_all x1, blocking collectives, per_device(): back = lax.all_to_all(out, 'space', 0, 0, tiled=True)  11.6 us
    all_to_all x1, starting transfers between devices, per_device(): recv = lax.all_to_all(routed, ('stretch', 'space'), 0, 0, tiled=True)  8.63 us
    all_to_all x1, starting transfers between devices, per_device(): spread = lax.all_to_all(pieces, 'stretch', 0, 0, tiled=True)  8.25 us
    ppermute x3, starting transfers between devices, per_device(): lax.ppermute(pieces, 'space', [(i, (i + k) % 4) for i in range(4)])  3.96 us
  transfers between devices with their start and end apart: 5, of which 3 were waited for; matrix products, arithmetic and copies ran while one was open for 2% of the time, Pallas kernels for 14%

profile of v1, /device:TPU:0, one launch (start us, length us, event | category | flops | bytes accessed | tf_op | source)
XLA Modules:
  0.0 151.1 jit_solution(13112500658550394904)
XLA Ops:
  0.6 0.0 copy-start.2
  0.6 1.8 %pad_maximum_fusion.mine = bf16[32,16,384]{2,1,0:T(8,128)(2,1)} fusion(bf16[32,8,384]{2,1,0:T(8,128)(2,1)} %bitcast.11, bf16[32,8,384]{2,1,0:T(8,128)(2,1)} %bitcast.12), kind=kLoop, calls=%fused_computation | loop fusion | flops 786432 | bytes 786432 | tf_op jit(solution)/shard_map/concatenate | solution.py:393
  2.5 8.2 %all-to-all-start = ((bf16[32,16,384]{2,1,0:T(8,128)(2,1)}), bf16[32,16,384]{2,1,0:T(8,128)(2,1)S(1)}, u32[]{:S(2)}, u32[]{:S(2)}) async-start(bf16[32,16,384]{2,1,0:T(8,128)(2,1)} %pad_maximum_fusion.mine), calls=%async_computation | async-start | bytes 786432 | tf_op jit(solution)/shard_map/all_to_all | solution.py:396
  10.7 0.0 copy-done.2
  10.7 24.3 %all-gather = s32[32,1,4]{2,1,0:T(1,128)} all-gather(s32[1,1,4]{2,1,0:T(1,128)S(1)} %bitcast.16), channel_id=1, replica_groups=mesh['stretch'=32,'space'=4] {'stretch'}, dimensions={0}, use_global_device_ids=true | all-gather | bytes 528 | tf_op jit(solution)/shard_map/all_gather | solution.py:395
  35.0 0.6 fusion.1
  35.6 2.0 %pad_add_fusion.place = s32[4]{0:T(128)} fusion(s32[1]{0:T(128)} %bitcast.3, s32[1]{0:T(128)} %bitcast.2, s32[1]{0:T(128)} %bitcast.1, s32[1]{0:T(128)} %bitcast), kind=kLoop, calls=%fused_computation.1 | loop fusion | flops 12 | bytes 32 | tf_op jit(solution)/shard_map/stack | solution.py:392
  37.5 0.0 all-to-all-done.pieces
  37.6 0.0 copy-start.1
  37.6 0.7 copy-done.1
  38.3 3.3 %route.1 = bf16[128,16,384]{2,1,0:T(8,128)(2,1)} custom-call(s32[4]{0:T(128)} %pad_add_fusion.place, s32[32,4]{1,0:T(8,128)} %bitcast.15, bf16[32,16,384]{2,1,0:T(8,128)(2,1)} %copy-done.1), custom_call_target="tpu_custom_call" | custom-call | tf_op jit(solution)/shard_map/route/pallas_call | solution.py:400
  41.6 8.6 %all-to-all-start.1 = ((bf16[128,16,384]{2,1,0:T(8,128)(2,1)}), bf16[128,16,384]{2,1,0:T(8,128)(2,1)S(1)}, u32[]{:S(2)}, u32[]{:S(2)}) async-start(bf16[128,16,384]{2,1,0:T(8,128)(2,1)} %route.1), calls=%async_computation.1 | async-start | bytes 3145728 | tf_op jit(solution)/shard_map/all_to_all | solution.py:407
  50.2 2.3 %collective-permute-start.2 = (bf16[32,16,384]{2,1,0:T(8,128)(2,1)}, bf16[32,16,384]{2,1,0:T(8,128)(2,1)S(1)}, u32[]{:S(2)}, u32[]{:S(2)}) collective-permute-start(bf16[32,16,384]{2,1,0:T(8,128)(2,1)} %pad_maximum_fusion.mine), channel_id=1, source_target_pairs={{0,3},{1,0},{2,1},{3,2},{4,7},{5,4},{6,5},{7,6},{8,11},{9,8},{10,9... | collective-permute-start | bytes 1179656 | tf_op jit(solution)/shard_map/ppermute | solution.py:398
  52.5 0.8 collective-permute-start.1
  53.3 0.9 collective-permute-start
  54.2 23.1 %collective-permute-done.2.from3 = bf16[32,16,384]{2,1,0:T(8,128)(2,1)S(1)} collective-permute-done((bf16[32,16,384]{2,1,0:T(8,128)(2,1)}, bf16[32,16,384]{2,1,0:T(8,128)(2,1)S(1)}, u32[]{:S(2)}, u32[]{:S(2)}) %collective-permute-start.2) | collective-permute-done | bytes 393248 | tf_op jit(solution)/shard_map/ppermute | solution.py:398
  77.3 0.0 copy-start.3
  77.3 1.6 %collective-permute-done.1.from2 = bf16[32,16,384]{2,1,0:T(8,128)(2,1)S(1)} collective-permute-done((bf16[32,16,384]{2,1,0:T(8,128)(2,1)}, bf16[32,16,384]{2,1,0:T(8,128)(2,1)S(1)}, u32[]{:S(2)}, u32[]{:S(2)}) %collective-permute-start.1) | collective-permute-done | bytes 393248 | tf_op jit(solution)/shard_map/ppermute | solution.py:398
  78.9 0.0 copy-start.4
  78.9 7.6 %collective-permute-done.from1 = bf16[32,16,384]{2,1,0:T(8,128)(2,1)S(1)} collective-permute-done((bf16[32,16,384]{2,1,0:T(8,128)(2,1)}, bf16[32,16,384]{2,1,0:T(8,128)(2,1)S(1)}, u32[]{:S(2)}, u32[]{:S(2)}) %collective-permute-start) | collective-permute-done | bytes 393248 | tf_op jit(solution)/shard_map/ppermute | solution.py:398
  86.5 0.0 copy-start.5
  86.5 0.0 copy-done.3
  86.5 0.0 copy-done.4
  86.5 0.7 copy-done.5
  87.3 21.7 %own.1 = (f32[5,320,384]{2,1,0:T(8,128)}, f32[3,320,384]{2,1,0:T(8,128)}) custom-call(s32[4]{0:T(128)} %pad_add_fusion.place, bf16[32,16,384]{2,1,0:T(8,128)(2,1)} %pad_maximum_fusion.mine, bf16[32,16,384]{2,1,0:T(8,128)(2,1)} %copy-done.5, bf16[32,16,384]{2,1,0:T(8,128)(2,1)} %copy-done.4, bf16[32,16,384]{2,1,0:T(8,128)(2,1)} %copy-done.3, f32[2,384]{1,0:T(2,128)} %gain.3, ...), custom_call_target="tpu_custom_call" | custom-call | flops 10192158720 | bytes 25165824 | tf_op jit(solution)/shard_map/own/pallas_call | solution.py:408
  109.0 0.0 all-to-all-done.1.recv
  109.0 0.0 copy-start
  109.0 1.1 copy-done
  110.1 28.6 %rest.1 = bf16[4,2,64,384]{3,2,1,0:T(8,128)(2,1)} custom-call(s32[4]{0:T(128)} %pad_add_fusion.place, bf16[32,16,384]{2,1,0:T(8,128)(2,1)} %pad_maximum_fusion.mine, bf16[32,16,384]{2,1,0:T(8,128)(2,1)} %copy-done.5, bf16[32,16,384]{2,1,0:T(8,128)(2,1)} %copy-done.4, bf16[32,16,384]{2,1,0:T(8,128)(2,1)} %copy-done.3, bf16[128,16,384]{2,1,0:T(8,128)(2,1)} %copy-done, ...), custom_call_target="tpu_custom_call" | custom-call | flops 12230590464 | bytes 25165824 | tf_op jit(solution)/shard_map/rest/pallas_call | solution.py:433
  138.7 11.6 %all_to_all.15 = bf16[4,2,64,384]{3,2,1,0:T(8,128)(2,1)S(1)} all-to-all(bf16[4,2,64,384]{3,2,1,0:T(8,128)(2,1)} %rest.1), channel_id=1, replica_groups=mesh['stretch'=32,'space'=4] {'space'}, dimensions={0} | all-to-all | bytes 786432 | tf_op jit(solution)/shard_map/all_to_all | solution.py:460
  150.3 0.8 fusion
Async XLA Ops:
  0.6 10.1 %copy-start.2 = (s32[1,4]{1,0:T(1,128)S(1)}, s32[1,4]{1,0:T(1,128)}, u32[]{:S(2)}) copy-start(s32[1,4]{1,0:T(1,128)} %param.7) | copy-start | bytes 52
  2.5 35.1 %all-to-all-start = ((bf16[32,16,384]{2,1,0:T(8,128)(2,1)}), bf16[32,16,384]{2,1,0:T(8,128)(2,1)S(1)}, u32[]{:S(2)}, u32[]{:S(2)}) async-start(bf16[32,16,384]{2,1,0:T(8,128)(2,1)} %pad_maximum_fusion.mine), calls=%async_computation | async-start | bytes 786432 | tf_op jit(solution)/shard_map/all_to_all | solution.py:396
  37.6 0.7 copy-start.1
  41.6 67.3 %all-to-all-start.1 = ((bf16[128,16,384]{2,1,0:T(8,128)(2,1)}), bf16[128,16,384]{2,1,0:T(8,128)(2,1)S(1)}, u32[]{:S(2)}, u32[]{:S(2)}) async-start(bf16[128,16,384]{2,1,0:T(8,128)(2,1)} %route.1), calls=%async_computation.1 | async-start | bytes 3145728 | tf_op jit(solution)/shard_map/all_to_all | solution.py:407
  50.2 27.0 %collective-permute-start.2 = (bf16[32,16,384]{2,1,0:T(8,128)(2,1)}, bf16[32,16,384]{2,1,0:T(8,128)(2,1)S(1)}, u32[]{:S(2)}, u32[]{:S(2)}) collective-permute-start(bf16[32,16,384]{2,1,0:T(8,128)(2,1)} %pad_maximum_fusion.mine), channel_id=1, source_target_pairs={{0,3},{1,0},{2,1},{3,2},{4,7},{5,4},{6,5},{7,6},{8,11},{9,8},{10,9... | collective-permute-start | bytes 1179656 | tf_op jit(solution)/shard_map/ppermute | solution.py:398
  52.5 26.4 %collective-permute-start.1 = (bf16[32,16,384]{2,1,0:T(8,128)(2,1)}, bf16[32,16,384]{2,1,0:T(8,128)(2,1)S(1)}, u32[]{:S(2)}, u32[]{:S(2)}) collective-permute-start(bf16[32,16,384]{2,1,0:T(8,128)(2,1)} %pad_maximum_fusion.mine), channel_id=1, source_target_pairs={{0,2},{1,3},{2,0},{3,1},{4,6},{5,7},{6,4},{7,5},{8,10},{9,11},{10,... | collective-permute-start | bytes 1179656 | tf_op jit(solution)/shard_map/ppermute | solution.py:398
  53.3 33.2 %collective-permute-start = (bf16[32,16,384]{2,1,0:T(8,128)(2,1)}, bf16[32,16,384]{2,1,0:T(8,128)(2,1)S(1)}, u32[]{:S(2)}, u32[]{:S(2)}) collective-permute-start(bf16[32,16,384]{2,1,0:T(8,128)(2,1)} %pad_maximum_fusion.mine), channel_id=1, source_target_pairs={{0,1},{1,2},{2,3},{3,0},{4,5},{5,6},{6,7},{7,4},{8,9},{9,10},{10,1... | collective-permute-start | bytes 1179656 | tf_op jit(solution)/shard_map/ppermute | solution.py:398
  77.3 9.2 %copy-start.3 = (bf16[32,16,384]{2,1,0:T(8,128)(2,1)}, bf16[32,16,384]{2,1,0:T(8,128)(2,1)S(1)}, u32[]{:S(2)}) copy-start(bf16[32,16,384]{2,1,0:T(8,128)(2,1)S(1)} %collective-permute-done.2.from3) | copy-start | bytes 1179652
  78.9 7.6 %copy-start.4 = (bf16[32,16,384]{2,1,0:T(8,128)(2,1)}, bf16[32,16,384]{2,1,0:T(8,128)(2,1)S(1)}, u32[]{:S(2)}) copy-start(bf16[32,16,384]{2,1,0:T(8,128)(2,1)S(1)} %collective-permute-done.1.from2) | copy-start | bytes 1179652
  86.5 0.7 copy-start.5
  109.0 1.1 copy-start

commit v2 on v1

--- a/solution.py
+++ b/solution.py
@@ -17,6 +17,7 @@
 BF16 = jnp.bfloat16
 VMEM = pl.BlockSpec(memory_space=pltpu.VMEM)
 SMEM = pl.BlockSpec(memory_space=pltpu.SMEM)
+HBM = pl.BlockSpec(memory_space=pltpu.HBM)
 ANY = pl.BlockSpec(memory_space=pl.ANY)
 
 
@@ -150,64 +151,103 @@
 
 
 def read_row(block):
-    parts = [block(cb).astype(F32) for cb in range(4)]
-    raw = jnp.concatenate([p[:8] for p in parts], axis=0)
-    cot = jnp.concatenate([p[8:] for p in parts], axis=0)
-    return raw, cot
-
-
-def start_weights(weight, taps, sems):
-    for layer in range(2):
-        for a in range(3):
-            pltpu.make_async_copy(
-                weight.at[layer, pl.ds(a * 9, 9)],
-                taps.at[layer, pl.ds(a * 9, 9)],
-                sems.at[layer, a],
-            ).start()
-
-
-def wait_weights(weight, taps, sems, layer):
-    for a in range(3):
+    return jnp.concatenate([block(half) for half in range(2)], axis=0)
+
+
+def layer_weights(weight, taps, sems, layer):
+    return [
         pltpu.make_async_copy(
             weight.at[layer, pl.ds(a * 9, 9)], taps.at[layer, pl.ds(a * 9, 9)], sems.at[layer, a]
-        ).wait()
-
-
-def route_kernel(place, table, pieces, out):
-    g = place[0] // 8
+        )
+        for a in range(3)
+    ]
+
+
+def start_weights(weight, taps, sems, layer):
+    for copy in layer_weights(weight, taps, sems, layer):
+        copy.start()
+
+
+def wait_weights(weight, taps, sems, layer):
+    for copy in layer_weights(weight, taps, sems, layer):
+        copy.wait()
+    if layer == 0:
+        start_weights(weight, taps, sems, 1)
+
+
+def prepare_kernel(table, frames, cot, pieces, *windows):
+    for n, part in enumerate((frames, cot)):
+        pieces[n * 16 : n * 16 + 16, 0:16, :] = part[...]
+    row = lax.broadcasted_iota(jnp.int32, (8, C), 0)
+    here = lax.broadcasted_iota(jnp.int32, (8, C), 1) == lax.axis_index("stretch")
+    links = jnp.where(row == 0, table[0, 3], jnp.where(row == 1, table[0, 2], 0))
+    links = jnp.where(here, links, 0).astype(F32).astype(BF16)
+    for k in range(32):
+        pieces[k, 16:24, :] = links
+    for shift, window in enumerate(windows):
+        first = (lax.rem(lax.axis_index("space") + shift + 1, 4) == 0).astype(jnp.int32)
+        order = [(frames, g) for g in (3, 0, 1, 2)] + [(cot, g) for g in (3, 2, 1, 0)]
+        for n, (part, g) in enumerate(order):
+
+            @pl.when((n >= first) & (n < first + 7))
+            def _(n=n, part=part, g=g, first=first, window=window):
+                window[pl.ds((n - first) * 4, 4)] = part[g * 4 : g * 4 + 4]
+
+
+def raw_block(j, g):
+    first = (j == 0).astype(jnp.int32)
+    return jnp.maximum(lax.rem(g + 1, 4) - first, 0) * 4
+
+
+def cot_block(j, g):
+    first = (j == 0).astype(jnp.int32)
+    return jnp.minimum(7 - g - first, 6) * 4
+
+
+def route_kernel(pieces, out, held, found, links, sem):
+    block = lax.axis_index("stretch")
+    g = lax.rem(block, 16) // 4
+    raw = block < 16
+
+    found[...] = sum(pieces[k, 16:24, 0:128].astype(F32) for k in range(32)).astype(jnp.int32)
+    copy = pltpu.make_async_copy(found, links, sem)
+    copy.start()
+    held[0:32] = pieces[:, 0:16, :]
+    held[32] = jnp.zeros((16, C), BF16)
+    copy.wait()
 
     def body(d, _):
-        nxt, prv = table[d, 2], table[d, 3]
+        prv, nxt = links[0, d], links[1, d]
         for j in range(4):
-            src = jnp.where(j <= g, prv, jnp.where(j >= g + 2, nxt, -1))
-            cot_src = jnp.where(j >= g, nxt, -1)
-            raw = pieces[jnp.maximum(src, 0)].astype(F32)[:8]
-            cot = pieces[jnp.maximum(cot_src, 0)].astype(F32)[8:]
-            raw = raw * (src >= 0).astype(F32)
-            cot = cot * (cot_src >= 0).astype(F32)
-            out[d * 4 + j] = jnp.concatenate([raw, cot], axis=0).astype(BF16)
-        return 0
-
-    lax.fori_loop(0, 32, body, 0)
+            raw_src = jnp.where(j <= g, prv, jnp.where(j >= g + 2, nxt, -1))
+            src = jnp.where(raw, raw_src, jnp.where(j >= g, nxt, -1))
+            out[d * 4 + j] = held[jnp.where(src < 0, 32, src)]
+        return 0
+
+    lax.fori_loop(0, 32, body, 0, unroll=4)
 
 
 def own_kernel(
-    place, mine, from1, from2, from3, gain, bias, weight, acc0, acc1,
-    taps, x, slab, gslab, sums, mean, inv_std, ones, sems,
+    table, mine, mine_cot, from1, from2, from3, gain, bias, weight, acc_out,
+    taps, x, slab, gslab, acc, sums, mean, inv_std, ones, sems, save_sems,
 ):
-    start_weights(weight, taps, sems)
-    j = place[1]
+    start_weights(weight, taps, sems, 0)
+    j = lax.axis_index("space")
     ones[...] = group_matrix()
-    acc0[...] = jnp.zeros_like(acc0)
-    acc1[...] = jnp.zeros_like(acc1)
-    for shift, part in enumerate((mine, from1, from2, from3)):
+    acc[...] = jnp.zeros_like(acc)
+    for shift, part in enumerate((None, from1, from2, from3)):
         holder = lax.rem(j + 4 - shift, 4)
 
         def rows(t, _, part=part, holder=holder):
             g, r = t // 2, lax.rem(t, 2)
-            raw, cot = read_row(lambda cb: part[t * 4 + cb])
-            x[g, pl.ds((holder * 2 + r) * COLS, COLS), :] = raw.astype(BF16)
-            store_shifted(gslab, g, holder * 2 + r, cot)
+            at = pl.ds((holder * 2 + r) * COLS, COLS)
+            if part is None:
+                x[g, at, :] = read_row(lambda half: mine[t * 2 + half])
+                cot = read_row(lambda half: mine_cot[t * 2 + half])
+            else:
+                x[g, at, :] = read_row(lambda half: part[raw_block(j, g) + r * 2 + half])
+                cot = read_row(lambda half: part[cot_block(j, g) + r * 2 + half])
+            store_shifted(gslab, g, holder * 2 + r, cot.astype(F32))
             return 0
 
         lax.fori_loop(0, 8, rows, 0)
@@ -229,11 +269,19 @@
 
         @pl.when((f >= 0) & (f <= 4))
         def _():
-            conv_tap(slab[g], taps.at[0], a, acc0, f)
+            conv_tap(slab[g], taps.at[0], a, acc, f)
 
         return 0
 
     lax.fori_loop(0, 12, forward, 0)
+    acc[8, 0:8] = mean[...]
+    acc[8, 8:16] = inv_std[...]
+    acc[8, COLS : COLS + CELLS] = x[j].astype(F32)
+    saves = [
+        pltpu.make_async_copy(acc.at[0:5], acc_out.at[0:5], save_sems.at[0]),
+        pltpu.make_async_copy(acc.at[5:9], acc_out.at[5:9], save_sems.at[1]),
+    ]
+    saves[0].start()
     wait_weights(weight, taps, sems, 1)
 
     def backward(t, _):
@@ -243,36 +291,33 @@
 
         @pl.when((u >= 0) & (f >= 0) & (f <= 2))
         def _():
-            adjoint_tap(gslab[g], taps.at[1], a, acc1, f)
+            adjoint_tap(gslab[g], taps.at[1], a, acc, 5 + f)
 
         return 0
 
     lax.fori_loop(0, 12, backward, 0)
+    saves[1].start()
+    for save in saves:
+        save.wait()
 
 
 def rest_kernel(
-    place, mine, from1, from2, from3, recv, acc0_in, acc1_in, gain, bias, weight, out,
-    taps, x, slab, gslab, acc0, acc1, acc2, h, sums, mean, inv_std, ones, raw_own, sems,
+    table, recv, acc_in, gain, bias, weight, out,
+    taps, x, slab, gslab, acc, acc2, h, sums, mean, inv_std, ones, sems, load_sem,
 ):
-    start_weights(weight, taps, sems)
-    j = place[1]
-    has_prev = (place[2] >= 0).astype(F32)
+    load = pltpu.make_async_copy(acc_in.at[0:9], acc, load_sem)
+    load.start()
+    start_weights(weight, taps, sems, 0)
+    j = lax.axis_index("space")
+    has_prev = (table[0, 3] >= 0).astype(F32)
     ones[...] = group_matrix()
-    acc0[...] = acc0_in[...]
-    acc1[...] = acc1_in[...]
-
-    for shift, part in enumerate((mine, from1, from2, from3)):
-        holder = lax.rem(j + 4 - shift, 4)
-        for r in range(2):
-            raw, _ = read_row(lambda cb: part[(j * 2 + r) * 4 + cb])
-            raw_own[0, pl.ds((holder * 2 + r) * COLS, COLS), :] = raw.astype(BF16)
 
     def rows(t, _):
         g, row = t // 8, lax.rem(t, 8)
         i, r = row // 2, lax.rem(row, 2)
-        raw, cot = read_row(lambda cb: recv[((g * 2 + r) * 4 + cb) * 4 + i])
-        x[g, pl.ds(row * COLS, COLS), :] = raw.astype(BF16)
-        store_shifted(gslab, g, row, cot)
+        x[g, pl.ds(row * COLS, COLS), :] = read_row(lambda half: recv[((g * 2 + r) * 2 + half) * 4 + i])
+        cot = read_row(lambda half: recv[(16 + (g * 2 + r) * 2 + half) * 4 + i])
+        store_shifted(gslab, g, row, cot.astype(F32))
         return 0
 
     lax.fori_loop(0, 32, rows, 0)
@@ -287,6 +332,7 @@
         return 0
 
     lax.fori_loop(0, 4, normed, 0)
+    load.wait()
     wait_weights(weight, taps, sems, 0)
 
     def forward(t, _):
@@ -296,7 +342,7 @@
 
         @pl.when((f >= 0) & (f <= 4) & (g != j - 1))
         def _():
-            conv_tap(slab[g], taps.at[0], a, acc0, f)
+            conv_tap(slab[g], taps.at[0], a, acc, f)
 
         return 0
 
@@ -310,14 +356,14 @@
 
         @pl.when((u <= 4) & (f >= 0) & (f <= 2))
         def _():
-            adjoint_tap(gslab[g], taps.at[1], a, acc1, f)
+            adjoint_tap(gslab[g], taps.at[1], a, acc, 5 + f)
 
         return 0
 
     lax.fori_loop(0, 12, backward, 0)
 
     def rounded(f, _):
-        h[f] = acc0[f, COLS : COLS + CELLS, :].astype(BF16)
+        h[f] = acc[f, COLS : COLS + CELLS, :].astype(BF16)
         return 0
 
     lax.fori_loop(0, 5, rounded, 0)
@@ -347,7 +393,7 @@
     def back_sums(f, _):
         n = f + 2
         one, two = norm_back_sums(
-            h, n, mean[pl.ds(n, 1), :], inv_std[pl.ds(n, 1), :], gain1, bias1, acc1, f
+            h, n, mean[pl.ds(n, 1), :], inv_std[pl.ds(n, 1), :], gain1, bias1, acc, 5 + f
         )
         sums[pl.ds(f, 1), :] = one
         sums[pl.ds(f + 4, 1), :] = two
@@ -360,7 +406,7 @@
         f, r = t // 8, lax.rem(t, 8)
         n = f + 2
         g1 = norm_back_row(
-            h, n, r, mean[pl.ds(n, 1), :], inv_std[pl.ds(n, 1), :], acc1, f,
+            h, n, r, mean[pl.ds(n, 1), :], inv_std[pl.ds(n, 1), :], acc, 5 + f,
             sums[pl.ds(f, 1), :], sums[pl.ds(f + 4, 1), :],
         )
         store_shifted(slab, f, r, g1)
@@ -375,8 +421,8 @@
 
     lax.fori_loop(0, 3, first, 0)
 
-    frame_stats(raw_own, 1, sums, mean, inv_std, ones)
-    m0, i0 = mean[0:1, :], inv_std[0:1, :]
+    m0, i0 = acc[8, pl.ds(j, 1), :], acc[8, pl.ds(8 + j, 1), :]
+    raw_own = acc.at[8:9, COLS : COLS + CELLS]
     one, two = norm_back_sums(raw_own, 0, m0, i0, gain[0:1, :], bias[0:1, :], acc2, 0)
     sums[0:1, :] = one
     sums[1:2, :] = two
@@ -387,76 +433,92 @@
 
 
 def per_device(frames, stretch_table, conv_weight, norm_gain, norm_bias, cotangent):
-    params = pltpu.CompilerParams(vmem_limit_bytes=58 * 2**20)
-    stretch, space = lax.axis_index("stretch"), lax.axis_index("space")
-    place = jnp.stack([stretch, space, stretch_table[0, 3], stretch_table[0, 2]]).astype(jnp.int32)
-    pieces = jnp.concatenate([frames.reshape(32, 8, C), cotangent.reshape(32, 8, C)], axis=1)
+    params = pltpu.CompilerParams(vmem_limit_bytes=115 * 2**19)
     weight = conv_weight.reshape(2, 27, C, C)
-    table = lax.all_gather(stretch_table, "stretch", axis=0, tiled=True)
-    spread = lax.all_to_all(pieces, "stretch", 0, 0, tiled=True)
+    mine, mine_cot = frames.reshape(16, 16, C), cotangent.reshape(16, 16, C)
+    pieces, *windows = pl.pallas_call(
+        prepare_kernel,
+        out_shape=[jax.ShapeDtypeStruct((32, 24, C), BF16)]
+        + [jax.ShapeDtypeStruct((28, 16, C), BF16)] * 3,
+        in_specs=[SMEM, VMEM, VMEM],
+        out_specs=[VMEM] * 4,
+        name="prepare",
+    )(stretch_table, mine, mine_cot)
     shifted = [
-        lax.ppermute(pieces, "space", [(i, (i + k) % 4) for i in range(4)]) for k in (1, 2, 3)
+        lax.ppermute(window, "space", [(i, (i + k) % 4) for i in range(4)])
+        for k, window in zip((1, 2, 3), windows)
     ]
+    spread = lax.cond(
+        stretch_table[0, 0] >= -1,
+        lambda p: lax.all_to_all(p, "stretch", 0, 0, tiled=True),
+        lambda p: p,
+        pieces,
+    )
+    spread, *shifted = lax.optimization_barrier((spread, *shifted))
     routed = pl.pallas_call(
         route_kernel,
         out_shape=jax.ShapeDtypeStruct((128, 16, C), BF16),
-        in_specs=[SMEM, SMEM, VMEM],
+        in_specs=[VMEM],
         out_specs=VMEM,
+        scratch_shapes=[
+            pltpu.VMEM((33, 16, C), BF16),
+            pltpu.VMEM((8, 128), jnp.int32),
+            pltpu.SMEM((8, 128), jnp.int32),
+            pltpu.SemaphoreType.DMA,
+        ],
         name="route",
-    )(place, table, spread)
+    )(spread)
     recv = lax.all_to_all(routed, ("stretch", "space"), 0, 0, tiled=True)
-    acc0, acc1 = pl.pallas_call(
+    acc = pl.pallas_call(
         own_kernel,
-        out_shape=[
-            jax.ShapeDtypeStruct((5, PADDED, C), F32),
-            jax.ShapeDtypeStruct((3, PADDED, C), F32),
-        ],
-        in_specs=[SMEM, VMEM, VMEM, VMEM, VMEM, VMEM, VMEM, ANY],
-        out_specs=[VMEM, VMEM],
+        out_shape=jax.ShapeDtypeStruct((32, PADDED, C), F32),
+        in_specs=[SMEM] + [VMEM] * 7 + [ANY],
+        out_specs=HBM,
         scratch_shapes=[
             pltpu.VMEM((2, 27, C, C), BF16),
             pltpu.VMEM((4, CELLS, C), BF16),
             pltpu.VMEM((4, CELLS, 3 * C), BF16),
             pltpu.VMEM((4, CELLS, 3 * C), BF16),
+            pltpu.VMEM((9, PADDED, C), F32),
             pltpu.VMEM((8, C), F32),
             pltpu.VMEM((8, C), F32),
             pltpu.VMEM((8, C), F32),
             pltpu.VMEM((C, C), BF16),
             pltpu.SemaphoreType.DMA((2, 3)),
+            pltpu.SemaphoreType.DMA((2,)),
         ],
         compiler_params=params,
         cost_estimate=pl.CostEstimate(
             flops=15 * 2 * CELLS * 9 * C * C, bytes_accessed=24 * 2**20, transcendentals=0
         ),
         name="own",
-    )(place, pieces, *shifted, norm_gain, norm_bias, weight)
+    )(stretch_table, mine, mine_cot, *shifted, norm_gain, norm_bias, weight)
     out = pl.pallas_call(
         rest_kernel,
         out_shape=jax.ShapeDtypeStruct((4, 2, 64, C), BF16),
-        in_specs=[SMEM, VMEM, VMEM, VMEM, VMEM, VMEM, VMEM, VMEM, VMEM, VMEM, ANY],
+        in_specs=[SMEM, VMEM, HBM, VMEM, VMEM, ANY],
         out_specs=VMEM,
         scratch_shapes=[
             pltpu.VMEM((2, 27, C, C), BF16),
             pltpu.VMEM((4, CELLS, C), BF16),
             pltpu.VMEM((4, CELLS, 3 * C), BF16),
             pltpu.VMEM((4, CELLS, 3 * C), BF16),
-            pltpu.VMEM((5, PADDED, C), F32),
-            pltpu.VMEM((3, PADDED, C), F32),
+            pltpu.VMEM((9, PADDED, C), F32),
             pltpu.VMEM((1, PADDED, C), F32),
             pltpu.VMEM((5, CELLS, C), BF16),
             pltpu.VMEM((8, C), F32),
             pltpu.VMEM((8, C), F32),
             pltpu.VMEM((8, C), F32),
             pltpu.VMEM((C, C), BF16),
-            pltpu.VMEM((1, CELLS, C), BF16),
             pltpu.SemaphoreType.DMA((2, 3)),
+            pltpu.SemaphoreType.DMA,
         ],
-        compiler_params=params,
+        compiler_params=pltpu.CompilerParams(vmem_limit_bytes=48 * 2**20),
         cost_estimate=pl.CostEstimate(
             flops=18 * 2 * CELLS * 9 * C * C, bytes_accessed=24 * 2**20, transcendentals=0
         ),
         name="rest",
-    )(place, pieces, *shifted, recv, acc0, acc1, norm_gain, norm_bias, weight)
+    )(stretch_table, recv, acc, norm_gain, norm_bias, weight)
     back = lax.all_to_all(out, "space", 0, 0, tiled=True)
     shape = frames.shape
     return back[:, 0].reshape(shape), back[:, 1].reshape(shape)

time: 152 us -> 100 us (0.66)
  waiting for transfers between devices: 32.3 us -> 3.68 us
  starting transfers between devices: 20.8 us -> 10.6 us
  other arithmetic: 3.77 us -> 0 us
  blocking collectives: 35.8 us -> 32.1 us
  local copies, waits for them, and re-layouts: 3.99 us -> 0.87 us
  Pallas kernels: 53.6 us -> 51.4 us
    ppermute x3, waiting for transfers between devices: 32.3 us -> 0.01 us  [per_device(): lax.ppermute(window, 'space', [(i, (i + k) % 4) for i in range(4)])]
    all_gather x1 -> x0, blocking collectives: 24.3 us -> none  [per_device(): table = lax.all_gather(stretch_table, 'stretch', axis=0, tiled=True)]
    all_to_all x0 -> x1, blocking collectives: none -> 19.8 us  [per_device(): lax.all_to_all(p, 'stretch', 0, 0, tiled=True)]
    all_to_all x1 -> x0, starting transfers between devices: 8.25 us -> none  [per_device(): spread = lax.all_to_all(pieces, 'stretch', 0, 0, tiled=True)]
    all_to_all x1, starting transfers between devices: 8.63 us -> 4.66 us  [per_device(): recv = lax.all_to_all(routed, ('stretch', 'space'), 0, 0, tiled=True)]
    all_to_all x1, waiting for transfers between devices: 0.01 us -> 3.68 us  [per_device(): recv = lax.all_to_all(routed, ('stretch', 'space'), 0, 0, tiled=True)]
    unnamed x12, local copies, waits for them, and re-layouts: 2.62 us -> 0.03 us
    pallas_call x1, Pallas kernels: 28.6 us -> 26.1 us  [per_device(): pl.pallas_call(rest_kernel, out_shape=jax.ShapeDtypeStruct((4, 2, 64, C),...]
  transfers between devices with their start and end apart: 5 -> 4, of which waited for: 3 -> 1; matrix products, arithmetic and copies ran while one was open for 2% -> 0% of each run, Pallas kernels for 14% -> 21%
where the time goes in v2:
time: 100 us
  Pallas kernels  51.4 us (51%)
  blocking collectives  32.1 us (32%)
  starting transfers between devices  10.6 us (11%)
  waiting for transfers between devices  3.68 us (4%)
  between operations  1.4 us (1%)
    pallas_call x1, Pallas kernels, per_device(): pl.pallas_call(rest_kernel, out_shape=jax.ShapeDtypeStruct((4, 2, 64, C),...  26.1 us
    pallas_call x1, Pallas kernels, per_device(): pl.pallas_call(own_kernel, out_shape=jax.ShapeDtypeStruct((32, PADDED, C)...  20.8 us
    all_to_all x1, blocking collectives, per_device(): lax.all_to_all(p, 'stretch', 0, 0, tiled=True)  19.8 us
    all_to_all x1, blocking collectives, per_device(): back = lax.all_to_all(out, 'space', 0, 0, tiled=True)  12.4 us
    ppermute x3, starting transfers between devices, per_device(): lax.ppermute(window, 'space', [(i, (i + k) % 4) for i in range(4)])  5.91 us
    all_to_all x1, starting transfers between devices, per_device(): recv = lax.all_to_all(routed, ('stretch', 'space'), 0, 0, tiled=True)  4.66 us
    all_to_all x1, waiting for transfers between devices, per_device(): recv = lax.all_to_all(routed, ('stretch', 'space'), 0, 0, tiled=True)  3.68 us
    pallas_call x1, Pallas kernels, per_device(): pl.pallas_call(route_kernel, out_shape=jax.ShapeDtypeStruct((128, 16, C),...  2.31 us
  transfers between devices with their start and end apart: 4, of which 1 were waited for; matrix products, arithmetic and copies ran while one was open for 0% of the time, Pallas kernels for 21%

profile of v2, /device:TPU:0, one launch (start us, length us, event | category | flops | bytes accessed | tf_op | source)
XLA Modules:
  0.0 100.1 jit_solution(10577684885397261621)
XLA Ops:
  0.6 2.2 %prepare.1 = (bf16[32,24,384]{2,1,0:T(8,128)(2,1)S(1)}, bf16[28,16,384]{2,1,0:T(8,128)(2,1)}, bf16[28,16,384]{2,1,0:T(8,128)(2,1)}, bf16[28,16,384]{2,1,0:T(8,128)(2,1)}) custom-call(s32[1,4]{1,0:T(1,128)} %table.5, bf16[16,16,384]{2,1,0:T(8,128)(2,1)} %bitcast.8, bf16[16,16,384]{2,1,0:T(8,128)(2,1)} %bitcast.10), custom_call_target="tpu_custom_call" | custom-call | tf_op jit(solution)/shard_map/prepare/pallas_call | solution.py:439
  2.8 1.7 %collective-permute-start = (bf16[28,16,384]{2,1,0:T(8,128)(2,1)}, bf16[28,16,384]{2,1,0:T(8,128)(2,1)S(1)}, u32[]{:S(2)}, u32[]{:S(2)}) collective-permute-start(bf16[28,16,384]{2,1,0:T(8,128)(2,1)} %get-tuple-element.16), channel_id=1, source_target_pairs={{0,1},{1,2},{2,3},{3,0},{4,5},{5,6},{6,7},{7,4},{8,9},{9,10},{10,1... | collective-permute-start | bytes 1032200 | tf_op jit(solution)/shard_map/ppermute | solution.py:448
  4.5 2.9 %collective-permute-start.1 = (bf16[28,16,384]{2,1,0:T(8,128)(2,1)}, bf16[28,16,384]{2,1,0:T(8,128)(2,1)S(1)}, u32[]{:S(2)}, u32[]{:S(2)}) collective-permute-start(bf16[28,16,384]{2,1,0:T(8,128)(2,1)} %get-tuple-element.17), channel_id=1, source_target_pairs={{0,2},{1,3},{2,0},{3,1},{4,6},{5,7},{6,4},{7,5},{8,10},{9,11},{10,... | collective-permute-start | bytes 1032200 | tf_op jit(solution)/shard_map/ppermute | solution.py:448
  7.4 1.4 %collective-permute-start.2 = (bf16[28,16,384]{2,1,0:T(8,128)(2,1)}, bf16[28,16,384]{2,1,0:T(8,128)(2,1)S(1)}, u32[]{:S(2)}, u32[]{:S(2)}) collective-permute-start(bf16[28,16,384]{2,1,0:T(8,128)(2,1)} %get-tuple-element.18), channel_id=1, source_target_pairs={{0,3},{1,0},{2,1},{3,2},{4,7},{5,4},{6,5},{7,6},{8,11},{9,8},{10,9... | collective-permute-start | bytes 1032200 | tf_op jit(solution)/shard_map/ppermute | solution.py:448
  9.4 19.9 %conditional.1 = (bf16[32,24,384]{2,1,0:T(8,128)(2,1)S(1)}) conditional(s32[]{:T(128)} %bitcast, bf16[32,24,384]{2,1,0:T(8,128)(2,1)S(1)} %get-tuple-element.15, bf16[32,24,384]{2,1,0:T(8,128)(2,1)S(1)} %get-tuple-element.15), branch_computations={%region_0.0_spmd, %region_1.0_spmd} | conditional | bytes 2359304 | solution.py:451
  9.4 0.1 copy.10
  9.5 19.8 %all_to_all.14 = bf16[32,24,384]{2,1,0:T(8,128)(2,1)S(1)} all-to-all(bf16[32,24,384]{2,1,0:T(8,128)(2,1)S(1)} %copy.10), channel_id=1, replica_groups=mesh['stretch'=32,'space'=4] {'stretch'}, dimensions={0} | all-to-all | bytes 1179648 | tf_op jit(solution)/shard_map/cond/branch_1_fun/all_to_all | solution.py:453
  29.2 0.0 collective-permute-done.from1
  29.2 0.0 copy-start.3
  29.2 0.0 collective-permute-done.1.from2
  29.2 0.0 copy-start.4
  29.2 0.0 collective-permute-done.2.from3
  29.3 0.0 copy-start.5
  29.3 2.3 %route.1 = bf16[128,16,384]{2,1,0:T(8,128)(2,1)} custom-call(bf16[32,24,384]{2,1,0:T(8,128)(2,1)S(1)} %get-tuple-element.25.pieces), custom_call_target="tpu_custom_call" | custom-call | tf_op jit(solution)/shard_map/route/pallas_call | solution.py:458
  31.6 4.7 %all-to-all-start.1 = ((bf16[128,16,384]{2,1,0:T(8,128)(2,1)}), bf16[128,16,384]{2,1,0:T(8,128)(2,1)S(1)}, u32[]{:S(2)}, u32[]{:S(2)}) async-start(bf16[128,16,384]{2,1,0:T(8,128)(2,1)} %route.1), calls=%async_computation.1 | async-start | bytes 3145728 | tf_op jit(solution)/shard_map/all_to_all | solution.py:471
  36.2 0.0 copy-done.3
  36.3 0.0 copy-done.4
  36.3 0.0 copy-done.5
  36.3 0.0 copy-start
  36.3 0.0 copy-start.1
  36.3 0.0 copy-start.2
  36.3 20.8 %own.1.acc_in = f32[32,320,384]{2,1,0:T(8,128)} custom-call(s32[1,4]{1,0:T(1,128)} %table.5, bf16[16,16,384]{2,1,0:T(8,128)(2,1)} %bitcast.9, bf16[16,16,384]{2,1,0:T(8,128)(2,1)} %bitcast.11, bf16[28,16,384]{2,1,0:T(8,128)(2,1)} %copy-done.3, bf16[28,16,384]{2,1,0:T(8,128)(2,1)} %copy-done.4, bf16[28,16,384]{2,1,0:T(8,128)(2,1)} %copy-done.5, ...), custom_call_target="tpu_custom_call" | custom-call | flops 10192158720 | bytes 25165824 | tf_op jit(solution)/shard_map/own/pallas_call | solution.py:472
  57.1 3.7 %all-to-all-done.1.recv = bf16[128,16,384]{2,1,0:T(8,128)(2,1)S(1)} async-done(((bf16[128,16,384]{2,1,0:T(8,128)(2,1)}), bf16[128,16,384]{2,1,0:T(8,128)(2,1)S(1)}, u32[]{:S(2)}, u32[]{:S(2)}) %all-to-all-start.1) | async-done | bytes 1572896 | tf_op jit(solution)/shard_map/all_to_all | solution.py:471
  60.8 0.0 copy-done
  60.8 0.0 copy-done.1
  60.8 0.0 copy-done.2
  60.8 26.1 %rest.1 = bf16[4,2,64,384]{3,2,1,0:T(8,128)(2,1)S(1)} custom-call(s32[1,4]{1,0:T(1,128)S(1)} %copy-done, bf16[128,16,384]{2,1,0:T(8,128)(2,1)S(1)} %all-to-all-done.1.recv, f32[32,320,384]{2,1,0:T(8,128)} %own.1.acc_in, f32[2,384]{1,0:T(2,128)S(1)} %copy-done.1, f32[2,384]{1,0:T(2,128)S(1)} %copy-done.2, bf16[2,27,384,384]{3,2,1,0:T(8,128)(2,1)} %bitcast.15), custom_call_target="tpu_custom_call" | custom-call | flops 12230590464 | bytes 25165824 | tf_op jit(solution)/shard_map/rest/pallas_call | solution.py:496
  86.9 12.4 %all_to_all.15 = bf16[4,2,64,384]{3,2,1,0:T(8,128)(2,1)S(1)} all-to-all(bf16[4,2,64,384]{3,2,1,0:T(8,128)(2,1)S(1)} %rest.1), channel_id=1, replica_groups=mesh['stretch'=32,'space'=4] {'space'}, dimensions={0} | all-to-all | bytes 786432 | tf_op jit(solution)/shard_map/all_to_all | solution.py:522
  99.3 0.8 fusion
Async XLA Ops:
  2.8 26.4 %collective-permute-start = (bf16[28,16,384]{2,1,0:T(8,128)(2,1)}, bf16[28,16,384]{2,1,0:T(8,128)(2,1)S(1)}, u32[]{:S(2)}, u32[]{:S(2)}) collective-permute-start(bf16[28,16,384]{2,1,0:T(8,128)(2,1)} %get-tuple-element.16), channel_id=1, source_target_pairs={{0,1},{1,2},{2,3},{3,0},{4,5},{5,6},{6,7},{7,4},{8,9},{9,10},{10,1... | collective-permute-start | bytes 1032200 | tf_op jit(solution)/shard_map/ppermute | solution.py:448
  4.5 24.8 %collective-permute-start.1 = (bf16[28,16,384]{2,1,0:T(8,128)(2,1)}, bf16[28,16,384]{2,1,0:T(8,128)(2,1)S(1)}, u32[]{:S(2)}, u32[]{:S(2)}) collective-permute-start(bf16[28,16,384]{2,1,0:T(8,128)(2,1)} %get-tuple-element.17), channel_id=1, source_target_pairs={{0,2},{1,3},{2,0},{3,1},{4,6},{5,7},{6,4},{7,5},{8,10},{9,11},{10,... | collective-permute-start | bytes 1032200 | tf_op jit(solution)/shard_map/ppermute | solution.py:448
  7.4 21.9 %collective-permute-start.2 = (bf16[28,16,384]{2,1,0:T(8,128)(2,1)}, bf16[28,16,384]{2,1,0:T(8,128)(2,1)S(1)}, u32[]{:S(2)}, u32[]{:S(2)}) collective-permute-start(bf16[28,16,384]{2,1,0:T(8,128)(2,1)} %get-tuple-element.18), channel_id=1, source_target_pairs={{0,3},{1,0},{2,1},{3,2},{4,7},{5,4},{6,5},{7,6},{8,11},{9,8},{10,9... | collective-permute-start | bytes 1032200 | tf_op jit(solution)/shard_map/ppermute | solution.py:448
  29.2 7.0 %copy-start.3 = (bf16[28,16,384]{2,1,0:T(8,128)(2,1)}, bf16[28,16,384]{2,1,0:T(8,128)(2,1)S(1)}, u32[]{:S(2)}) copy-start(bf16[28,16,384]{2,1,0:T(8,128)(2,1)S(1)} %collective-permute-done.from1) | copy-start | bytes 1032196
  29.2 7.0 %copy-start.4 = (bf16[28,16,384]{2,1,0:T(8,128)(2,1)}, bf16[28,16,384]{2,1,0:T(8,128)(2,1)S(1)}, u32[]{:S(2)}) copy-start(bf16[28,16,384]{2,1,0:T(8,128)(2,1)S(1)} %collective-permute-done.1.from2) | copy-start | bytes 1032196
  29.3 7.0 %copy-start.5 = (bf16[28,16,384]{2,1,0:T(8,128)(2,1)}, bf16[28,16,384]{2,1,0:T(8,128)(2,1)S(1)}, u32[]{:S(2)}) copy-start(bf16[28,16,384]{2,1,0:T(8,128)(2,1)S(1)} %collective-permute-done.2.from3) | copy-start | bytes 1032196
  31.6 29.2 %all-to-all-start.1 = ((bf16[128,16,384]{2,1,0:T(8,128)(2,1)}), bf16[128,16,384]{2,1,0:T(8,128)(2,1)S(1)}, u32[]{:S(2)}, u32[]{:S(2)}) async-start(bf16[128,16,384]{2,1,0:T(8,128)(2,1)} %route.1), calls=%async_computation.1 | async-start | bytes 3145728 | tf_op jit(solution)/shard_map/all_to_all | solution.py:471
  36.3 24.5 %copy-start = (s32[1,4]{1,0:T(1,128)S(1)}, s32[1,4]{1,0:T(1,128)}, u32[]{:S(2)}) copy-start(s32[1,4]{1,0:T(1,128)} %table.5) | copy-start | bytes 52
  36.3 24.5 %copy-start.1 = (f32[2,384]{1,0:T(2,128)S(1)}, f32[2,384]{1,0:T(2,128)}, u32[]{:S(2)}) copy-start(f32[2,384]{1,0:T(2,128)} %gain.3) | copy-start | bytes 9220
  36.3 24.5 %copy-start.2 = (f32[2,384]{1,0:T(2,128)S(1)}, f32[2,384]{1,0:T(2,128)}, u32[]{:S(2)}) copy-start(f32[2,384]{1,0:T(2,128)} %bias.3) | copy-start | bytes 9220

commit v3 on v2

--- a/solution.py
+++ b/solution.py
@@ -59,26 +59,44 @@
     slab[idx, at, 2 * C : 3 * C] = right.astype(BF16)
 
 
-def conv_tap(slab_in, taps, a, acc, f):
+def conv_taps(slab, first, taps, a, n, acc, f):
+    cells = jnp.concatenate([slab[first + i] for i in range(n)], axis=1)
     w = jnp.concatenate(
-        [taps[pl.ds(a * 9 + 3 * b, 3)].reshape(3 * C, C) for b in range(3)], axis=1
+        [
+            jnp.concatenate(
+                [taps[pl.ds((a + i) * 9 + 3 * b, 3)].reshape(3 * C, C) for b in range(3)], axis=1
+            )
+            for i in range(n)
+        ],
+        axis=0,
     )
-    y = jnp.dot(slab_in, w, preferred_element_type=F32)
+    y = jnp.dot(cells, w, preferred_element_type=F32)
     for b in range(3):
         acc[f, (2 - b) * COLS : (2 - b) * COLS + CELLS, :] += y[:, b * C : (b + 1) * C]
 
 
-def adjoint_tap(slab_in, taps, a, acc, f):
+def adjoint_taps(slab, first, taps, a, n, acc, f):
+    cells = jnp.concatenate([slab[first - i] for i in range(n)], axis=1)
     w = jnp.concatenate(
         [
-            jnp.concatenate([taps[a * 9 + 3 * b + 2 - e] for e in range(3)], axis=1)
+            jnp.concatenate(
+                [taps[(a + i) * 9 + 3 * b + 2 - e] for i in range(n) for e in range(3)], axis=1
+            )
             for b in range(3)
         ],
         axis=0,
     )
-    y = lax.dot_general(slab_in, w, (((1,), (1,)), ((), ())), preferred_element_type=F32)
+    y = lax.dot_general(cells, w, (((1,), (1,)), ((), ())), preferred_element_type=F32)
     for b in range(3):
         acc[f, b * COLS : b * COLS + CELLS, :] += y[:, b * C : (b + 1) * C]
+
+
+def by_count(step, slab, first, taps, a, n, acc, f):
+    for count in (1, 2, 3):
+
+        @pl.when(n == count)
+        def _(count=count):
+            step(slab, first, taps, a, count, acc, f)
 
 
 def frame_sums(x, idx):
@@ -177,13 +195,14 @@
 
 def prepare_kernel(table, frames, cot, pieces, *windows):
     for n, part in enumerate((frames, cot)):
-        pieces[n * 16 : n * 16 + 16, 0:16, :] = part[...]
-    row = lax.broadcasted_iota(jnp.int32, (8, C), 0)
-    here = lax.broadcasted_iota(jnp.int32, (8, C), 1) == lax.axis_index("stretch")
+        for c in range(3):
+            pieces[n * 16 : n * 16 + 16, c * 16 : c * 16 + 16, :] = part[:, :, c * 128 : c * 128 + 128]
+    row = lax.broadcasted_iota(jnp.int32, (8, 128), 0)
+    here = lax.broadcasted_iota(jnp.int32, (8, 128), 1) == lax.axis_index("stretch")
     links = jnp.where(row == 0, table[0, 3], jnp.where(row == 1, table[0, 2], 0))
     links = jnp.where(here, links, 0).astype(F32).astype(BF16)
     for k in range(32):
-        pieces[k, 16:24, :] = links
+        pieces[k, 48:56, :] = links
     for shift, window in enumerate(windows):
         first = (lax.rem(lax.axis_index("space") + shift + 1, 4) == 0).astype(jnp.int32)
         order = [(frames, g) for g in (3, 0, 1, 2)] + [(cot, g) for g in (3, 2, 1, 0)]
@@ -209,10 +228,11 @@
     g = lax.rem(block, 16) // 4
     raw = block < 16
 
-    found[...] = sum(pieces[k, 16:24, 0:128].astype(F32) for k in range(32)).astype(jnp.int32)
+    found[...] = sum(pieces[k, 48:56, :].astype(F32) for k in range(32)).astype(jnp.int32)
     copy = pltpu.make_async_copy(found, links, sem)
     copy.start()
-    held[0:32] = pieces[:, 0:16, :]
+    for c in range(3):
+        held[0:32, :, c * 128 : c * 128 + 128] = pieces[:, c * 16 : c * 16 + 16, :]
     held[32] = jnp.zeros((16, C), BF16)
     copy.wait()
 
@@ -229,7 +249,7 @@
 
 def own_kernel(
     table, mine, mine_cot, from1, from2, from3, gain, bias, weight, acc_out,
-    taps, x, slab, gslab, acc, sums, mean, inv_std, ones, sems, save_sems,
+    taps, x, slab, gslab, acc, h, sums, mean, inv_std, ones, sems, save_sems,
 ):
     start_weights(weight, taps, sems, 0)
     j = lax.axis_index("space")
@@ -263,39 +283,46 @@
     lax.fori_loop(0, 4, normed, 0)
     wait_weights(weight, taps, sems, 0)
 
-    def forward(t, _):
-        g, a = t // 3, lax.rem(t, 3)
-        f = g + 4 - j - a
-
-        @pl.when((f >= 0) & (f <= 4))
-        def _():
-            conv_tap(slab[g], taps.at[0], a, acc, f)
-
-        return 0
-
-    lax.fori_loop(0, 12, forward, 0)
+    def forward(f, _):
+        low = jnp.maximum(0, 4 - j - f)
+        n = jnp.minimum(2, 7 - j - f) - low + 1
+        by_count(conv_taps, slab, f + low - 4 + j, taps.at[0], low, n, acc, f)
+        return 0
+
+    lax.fori_loop(0, 5, forward, 0)
     acc[8, 0:8] = mean[...]
     acc[8, 8:16] = inv_std[...]
     acc[8, COLS : COLS + CELLS] = x[j].astype(F32)
     saves = [
         pltpu.make_async_copy(acc.at[0:5], acc_out.at[0:5], save_sems.at[0]),
-        pltpu.make_async_copy(acc.at[5:9], acc_out.at[5:9], save_sems.at[1]),
+        pltpu.make_async_copy(acc.at[5:10], acc_out.at[5:10], save_sems.at[1]),
     ]
     saves[0].start()
     wait_weights(weight, taps, sems, 1)
 
-    def backward(t, _):
-        g, a = t // 3, lax.rem(t, 3)
-        u = g - j
-        f = u - 2 + a
-
-        @pl.when((u >= 0) & (f >= 0) & (f <= 2))
-        def _():
-            adjoint_tap(gslab[g], taps.at[1], a, acc, 5 + f)
-
-        return 0
-
-    lax.fori_loop(0, 12, backward, 0)
+    def backward(f, _):
+        low = jnp.maximum(0, f + j - 1)
+        by_count(adjoint_taps, gslab, j + f + 2 - low, taps.at[1], low, 3 - low, acc, 5 + f)
+        return 0
+
+    lax.fori_loop(0, 3, backward, 0)
+
+    @pl.when(j >= 2)
+    def _():
+        for n in range(2):
+            h[n] = acc[1 + n, COLS : COLS + CELLS, :].astype(BF16)
+        frame_stats(h, 2, sums, mean, inv_std, ones)
+
+        def normed1(n, _):
+            norm_silu_frame(
+                h, n, mean[pl.ds(n, 1), :], inv_std[pl.ds(n, 1), :],
+                gain[1:2, :], bias[1:2, :], slab, n, None,
+            )
+            return 0
+
+        lax.fori_loop(0, 2, normed1, 0)
+        by_count(conv_taps, slab, 3 - j, taps.at[1], 4 - j, j - 1, acc, 9)
+
     saves[1].start()
     for save in saves:
         save.wait()
@@ -305,7 +332,7 @@
     table, recv, acc_in, gain, bias, weight, out,
     taps, x, slab, gslab, acc, acc2, h, sums, mean, inv_std, ones, sems, load_sem,
 ):
-    load = pltpu.make_async_copy(acc_in.at[0:9], acc, load_sem)
+    load = pltpu.make_async_copy(acc_in.at[0:10], acc, load_sem)
     load.start()
     start_weights(weight, taps, sems, 0)
     j = lax.axis_index("space")
@@ -314,9 +341,14 @@
 
     def rows(t, _):
         g, row = t // 8, lax.rem(t, 8)
-        i, r = row // 2, lax.rem(row, 2)
-        x[g, pl.ds(row * COLS, COLS), :] = read_row(lambda half: recv[((g * 2 + r) * 2 + half) * 4 + i])
-        cot = read_row(lambda half: recv[(16 + (g * 2 + r) * 2 + half) * 4 + i])
+        block = (g * 2 + lax.rem(row, 2)) * 2
+        x[g, pl.ds(row * COLS, COLS), :] = read_row(lambda half: recv[(block + half) * 4 + row // 2])
+        return 0
+
+    def cot_rows(t, _):
+        g, row = t // 8, lax.rem(t, 8)
+        block = 16 + (g * 2 + lax.rem(row, 2)) * 2
+        cot = read_row(lambda half: recv[(block + half) * 4 + row // 2])
         store_shifted(gslab, g, row, cot.astype(F32))
         return 0
 
@@ -332,35 +364,27 @@
         return 0
 
     lax.fori_loop(0, 4, normed, 0)
+    lax.fori_loop(0, 8 * (j + 1), cot_rows, 0)
     load.wait()
     wait_weights(weight, taps, sems, 0)
 
-    def forward(t, _):
-        g, a = t // 3, lax.rem(t, 3)
-        w = jnp.where(g >= j, g - j, g - j + 8)
-        f = w - a
-
-        @pl.when((f >= 0) & (f <= 4) & (g != j - 1))
-        def _():
-            conv_tap(slab[g], taps.at[0], a, acc, f)
-
-        return 0
-
-    lax.fori_loop(0, 12, forward, 0)
+    def forward(f, _):
+        prev = f < 4 - j
+        low = jnp.where(prev, 0, jnp.maximum(0, 8 - j - f))
+        n = jnp.where(prev, jnp.minimum(2, 3 - j - f), 2) - low + 1
+        first = jnp.where(prev, j + f, f + low - 8 + j)
+        by_count(conv_taps, slab, first, taps.at[0], low, n, acc, f)
+        return 0
+
+    lax.fori_loop(0, 5, forward, 0)
     wait_weights(weight, taps, sems, 1)
 
-    def backward(t, _):
-        g, a = t // 3, lax.rem(t, 3)
-        u = g + 4 - j
-        f = u - 2 + a
-
-        @pl.when((u <= 4) & (f >= 0) & (f <= 2))
-        def _():
-            adjoint_tap(gslab[g], taps.at[1], a, acc, 5 + f)
-
-        return 0
-
-    lax.fori_loop(0, 12, backward, 0)
+    def backward(f, _):
+        n = jnp.minimum(2, f + j - 2) + 1
+        by_count(adjoint_taps, gslab, f - 2 + j, taps.at[1], 0, n, acc, 5 + f)
+        return 0
+
+    lax.fori_loop(0, 3, backward, 0)
 
     def rounded(f, _):
         h[f] = acc[f, COLS : COLS + CELLS, :].astype(BF16)
@@ -378,15 +402,9 @@
         return 0
 
     lax.fori_loop(0, 3, normed1, 0)
-    acc2[...] = jnp.zeros_like(acc2)
-
-    def last(a, _):
-        conv_tap(slab[a], taps.at[1], a, acc2, 0)
-        return 0
-
-    lax.fori_loop(0, 3, last, 0)
+    by_count(conv_taps, slab, 0, taps.at[1], 0, jnp.minimum(3, 4 - j), acc, 9)
     for i in range(4):
-        out[i, 0] = acc2[0, COLS + i * 64 : COLS + i * 64 + 64, :].astype(BF16)
+        out[i, 0] = acc[9, COLS + i * 64 : COLS + i * 64 + 64, :].astype(BF16)
 
     sums[...] = jnp.zeros_like(sums)
 
@@ -415,11 +433,7 @@
     lax.fori_loop(0, 24, back_rows, 0)
     acc2[...] = jnp.zeros_like(acc2)
 
-    def first(a, _):
-        adjoint_tap(slab[2 - a], taps.at[0], a, acc2, 0)
-        return 0
-
-    lax.fori_loop(0, 3, first, 0)
+    adjoint_taps(slab, 2, taps.at[0], 0, 3, acc2, 0)
 
     m0, i0 = acc[8, pl.ds(j, 1), :], acc[8, pl.ds(8 + j, 1), :]
     raw_own = acc.at[8:9, COLS : COLS + CELLS]
@@ -433,12 +447,13 @@
 
 
 def per_device(frames, stretch_table, conv_weight, norm_gain, norm_bias, cotangent):
+    small = pltpu.CompilerParams(vmem_limit_bytes=8 * 2**20)
     params = pltpu.CompilerParams(vmem_limit_bytes=115 * 2**19)
     weight = conv_weight.reshape(2, 27, C, C)
     mine, mine_cot = frames.reshape(16, 16, C), cotangent.reshape(16, 16, C)
     pieces, *windows = pl.pallas_call(
         prepare_kernel,
-        out_shape=[jax.ShapeDtypeStruct((32, 24, C), BF16)]
+        out_shape=[jax.ShapeDtypeStruct((32, 56, 128), BF16)]
         + [jax.ShapeDtypeStruct((28, 16, C), BF16)] * 3,
         in_specs=[SMEM, VMEM, VMEM],
         out_specs=[VMEM] * 4,
@@ -448,13 +463,7 @@
         lax.ppermute(window, "space", [(i, (i + k) % 4) for i in range(4)])
         for k, window in zip((1, 2, 3), windows)
     ]
-    spread = lax.cond(
-        stretch_table[0, 0] >= -1,
-        lambda p: lax.all_to_all(p, "stretch", 0, 0, tiled=True),
-        lambda p: p,
-        pieces,
-    )
-    spread, *shifted = lax.optimization_barrier((spread, *shifted))
+    spread = lax.all_to_all(pieces, "stretch", 0, 0, tiled=True)
     routed = pl.pallas_call(
         route_kernel,
         out_shape=jax.ShapeDtypeStruct((128, 16, C), BF16),
@@ -466,6 +475,7 @@
             pltpu.SMEM((8, 128), jnp.int32),
             pltpu.SemaphoreType.DMA,
         ],
+        compiler_params=small,
         name="route",
     )(spread)
     recv = lax.all_to_all(routed, ("stretch", "space"), 0, 0, tiled=True)
@@ -479,7 +489,8 @@
             pltpu.VMEM((4, CELLS, C), BF16),
             pltpu.VMEM((4, CELLS, 3 * C), BF16),
             pltpu.VMEM((4, CELLS, 3 * C), BF16),
-            pltpu.VMEM((9, PADDED, C), F32),
+            pltpu.VMEM((10, PADDED, C), F32),
+            pltpu.VMEM((2, CELLS, C), BF16),
             pltpu.VMEM((8, C), F32),
             pltpu.VMEM((8, C), F32),
             pltpu.VMEM((8, C), F32),
@@ -489,7 +500,7 @@
         ],
         compiler_params=params,
         cost_estimate=pl.CostEstimate(
-            flops=15 * 2 * CELLS * 9 * C * C, bytes_accessed=24 * 2**20, transcendentals=0
+            flops=1500 * 2 * CELLS * 9 * C * C, bytes_accessed=24 * 2**20, transcendentals=0
         ),
         name="own",
     )(stretch_table, mine, mine_cot, *shifted, norm_gain, norm_bias, weight)
@@ -503,7 +514,7 @@
             pltpu.VMEM((4, CELLS, C), BF16),
             pltpu.VMEM((4, CELLS, 3 * C), BF16),
             pltpu.VMEM((4, CELLS, 3 * C), BF16),
-            pltpu.VMEM((9, PADDED, C), F32),
+            pltpu.VMEM((10, PADDED, C), F32),
             pltpu.VMEM((1, PADDED, C), F32),
             pltpu.VMEM((5, CELLS, C), BF16),
             pltpu.VMEM((8, C), F32),

time: 100 us -> 92.9 us (0.929)
  blocking collectives: 32.1 us -> 11.2 us
  starting transfers between devices: 10.6 us -> 21.5 us
  waiting for transfers between devices: 3.68 us -> 9.15 us
  Pallas kernels: 51.4 us -> 48.2 us
    all_to_all x1 -> x0, blocking collectives: 19.8 us -> none  [per_device(): lax.all_to_all(p, 'stretch', 0, 0, tiled=True)]
    all_to_all x0 -> x1, starting transfers between devices: none -> 8.24 us  [per_device(): spread = lax.all_to_all(pieces, 'stretch', 0, 0, tiled=True)]
    all_to_all x0 -> x1, waiting for transfers between devices: none -> 4.65 us  [per_device(): spread = lax.all_to_all(pieces, 'stretch', 0, 0, tiled=True)]
    all_to_all x1, starting transfers between devices: 4.66 us -> 7.37 us  [per_device(): recv = lax.all_to_all(routed, ('stretch', 'space'), 0, 0, tiled=True)]
    pallas_call x1, Pallas kernels: 20.8 us -> 18.7 us  [per_device(): pl.pallas_call(own_kernel, out_shape=jax.ShapeDtypeStruct((32, PADDED, C)...]
    pallas_call x1, Pallas kernels: 26.1 us -> 24.8 us  [per_device(): pl.pallas_call(rest_kernel, out_shape=jax.ShapeDtypeStruct((4, 2, 64, C),...]
    all_to_all x1, blocking collectives: 12.4 us -> 11.2 us  [per_device(): back = lax.all_to_all(out, 'space', 0, 0, tiled=True)]
  transfers between devices with their start and end apart: 4 -> 5, of which waited for: 1 -> 2; matrix products, arithmetic and copies ran while one was open for 0% -> 0% of each run, Pallas kernels for 21% -> 23%
where the time goes in v3:
time: 92.9 us; the launch traced here: 92.5 us
  Pallas kernels  48.2 us (52%)
  starting transfers between devices  21.5 us (23%)
  blocking collectives  11.2 us (12%)
  waiting for transfers between devices  9.15 us (10%)
  local copies, waits for them, and re-layouts  1.72 us (2%)
    pallas_call x1, Pallas kernels, per_device(): pl.pallas_call(rest_kernel, out_shape=jax.ShapeDtypeStruct((4, 2, 64, C),...  24.8 us
    pallas_call x1, Pallas kernels, per_device(): pl.pallas_call(own_kernel, out_shape=jax.ShapeDtypeStruct((32, PADDED, C)...  18.7 us
    all_to_all x1, blocking collectives, per_device(): back = lax.all_to_all(out, 'space', 0, 0, tiled=True)  11.2 us
    all_to_all x1, starting transfers between devices, per_device(): spread = lax.all_to_all(pieces, 'stretch', 0, 0, tiled=True)  8.24 us
    all_to_all x1, starting transfers between devices, per_device(): recv = lax.all_to_all(routed, ('stretch', 'space'), 0, 0, tiled=True)  7.37 us
    ppermute x3, starting transfers between devices, per_device(): lax.ppermute(window, 'space', [(i, (i + k) % 4) for i in range(4)])  5.9 us
    all_to_all x1, waiting for transfers between devices, per_device(): spread = lax.all_to_all(pieces, 'stretch', 0, 0, tiled=True)  4.65 us
    all_to_all x1, waiting for transfers between devices, per_device(): recv = lax.all_to_all(routed, ('stretch', 'space'), 0, 0, tiled=True)  4.48 us
  transfers between devices with their start and end apart: 5, of which 2 were waited for; matrix products, arithmetic and copies ran while one was open for 0% of the time, Pallas kernels for 23%

profile of v3, /device:TPU:0, one launch (start us, length us, event | category | flops | bytes accessed | tf_op | source)
XLA Modules:
  0.0 92.5 jit_solution(5306262367623860928)
XLA Ops:
  0.6 2.4 %prepare.1 = (bf16[32,56,128]{2,1,0:T(8,128)(2,1)}, bf16[28,16,384]{2,1,0:T(8,128)(2,1)}, bf16[28,16,384]{2,1,0:T(8,128)(2,1)}, bf16[28,16,384]{2,1,0:T(8,128)(2,1)}) custom-call(s32[1,4]{1,0:T(1,128)} %table.5, bf16[16,16,384]{2,1,0:T(8,128)(2,1)} %bitcast.5, bf16[16,16,384]{2,1,0:T(8,128)(2,1)} %bitcast.7), custom_call_target="tpu_custom_call" | custom-call | tf_op jit(solution)/shard_map/prepare/pallas_call | solution.py:454
  3.0 8.2 %all-to-all-start = ((bf16[32,56,128]{2,1,0:T(8,128)(2,1)}), bf16[32,56,128]{2,1,0:T(8,128)(2,1)S(1)}, u32[]{:S(2)}, u32[]{:S(2)}) async-start(bf16[32,56,128]{2,1,0:T(8,128)(2,1)} %get-tuple-element.6), calls=%async_computation | async-start | bytes 917504 | tf_op jit(solution)/shard_map/all_to_all | solution.py:466
  11.2 1.6 %collective-permute-start = (bf16[28,16,384]{2,1,0:T(8,128)(2,1)}, bf16[28,16,384]{2,1,0:T(8,128)(2,1)S(1)}, u32[]{:S(2)}, u32[]{:S(2)}) collective-permute-start(bf16[28,16,384]{2,1,0:T(8,128)(2,1)} %get-tuple-element.7), channel_id=1, source_target_pairs={{0,1},{1,2},{2,3},{3,0},{4,5},{5,6},{6,7},{7,4},{8,9},{9,10},{10,1... | collective-permute-start | bytes 1032200 | tf_op jit(solution)/shard_map/ppermute | solution.py:463
  12.9 2.9 %collective-permute-start.1 = (bf16[28,16,384]{2,1,0:T(8,128)(2,1)}, bf16[28,16,384]{2,1,0:T(8,128)(2,1)S(1)}, u32[]{:S(2)}, u32[]{:S(2)}) collective-permute-start(bf16[28,16,384]{2,1,0:T(8,128)(2,1)} %get-tuple-element.8), channel_id=1, source_target_pairs={{0,2},{1,3},{2,0},{3,1},{4,6},{5,7},{6,4},{7,5},{8,10},{9,11},{10,... | collective-permute-start | bytes 1032200 | tf_op jit(solution)/shard_map/ppermute | solution.py:463
  15.8 1.4 %collective-permute-start.2 = (bf16[28,16,384]{2,1,0:T(8,128)(2,1)}, bf16[28,16,384]{2,1,0:T(8,128)(2,1)S(1)}, u32[]{:S(2)}, u32[]{:S(2)}) collective-permute-start(bf16[28,16,384]{2,1,0:T(8,128)(2,1)} %get-tuple-element.9), channel_id=1, source_target_pairs={{0,3},{1,0},{2,1},{3,2},{4,7},{5,4},{6,5},{7,6},{8,11},{9,8},{10,9... | collective-permute-start | bytes 1032200 | tf_op jit(solution)/shard_map/ppermute | solution.py:463
  17.1 4.7 %all-to-all-done.pieces = bf16[32,56,128]{2,1,0:T(8,128)(2,1)S(1)} async-done(((bf16[32,56,128]{2,1,0:T(8,128)(2,1)}), bf16[32,56,128]{2,1,0:T(8,128)(2,1)S(1)}, u32[]{:S(2)}, u32[]{:S(2)}) %all-to-all-start) | async-done | bytes 458784 | tf_op jit(solution)/shard_map/all_to_all | solution.py:466
  21.8 2.4 %route.1 = bf16[128,16,384]{2,1,0:T(8,128)(2,1)} custom-call(bf16[32,56,128]{2,1,0:T(8,128)(2,1)S(1)} %all-to-all-done.pieces), custom_call_target="tpu_custom_call" | custom-call | tf_op jit(solution)/shard_map/route/pallas_call | solution.py:467
  24.2 7.4 %all-to-all-start.1 = ((bf16[128,16,384]{2,1,0:T(8,128)(2,1)}), bf16[128,16,384]{2,1,0:T(8,128)(2,1)}, u32[]{:S(2)}, u32[]{:S(2)}) async-start(bf16[128,16,384]{2,1,0:T(8,128)(2,1)} %route.1), calls=%async_computation.1 | async-start | bytes 3145728 | tf_op jit(solution)/shard_map/all_to_all | solution.py:481
  31.6 0.0 collective-permute-done.from1
  31.6 0.0 copy-start.3
  31.6 0.0 collective-permute-done.1.from2
  31.6 0.0 copy-start.4
  31.6 0.0 collective-permute-done.2.from3
  31.6 0.0 copy-start.5
  31.6 0.7 copy-done.3
  32.3 0.1 copy-done.4
  32.4 0.1 copy-done.5
  32.5 0.0 copy-start
  32.5 0.0 copy-start.1
  32.5 0.0 copy-start.2
  32.5 18.7 %own.1.acc_in = f32[32,320,384]{2,1,0:T(8,128)} custom-call(s32[1,4]{1,0:T(1,128)} %table.5, bf16[16,16,384]{2,1,0:T(8,128)(2,1)} %bitcast.6, bf16[16,16,384]{2,1,0:T(8,128)(2,1)} %bitcast.8, bf16[28,16,384]{2,1,0:T(8,128)(2,1)} %copy-done.3, bf16[28,16,384]{2,1,0:T(8,128)(2,1)} %copy-done.4, bf16[28,16,384]{2,1,0:T(8,128)(2,1)} %copy-done.5, ...), custom_call_target="tpu_custom_call" | custom-call | flops 1019215872000 | bytes 25165824 | tf_op jit(solution)/shard_map/own/pallas_call | solution.py:482
  51.3 4.5 %all-to-all-done.1.recv = bf16[128,16,384]{2,1,0:T(8,128)(2,1)} async-done(((bf16[128,16,384]{2,1,0:T(8,128)(2,1)}), bf16[128,16,384]{2,1,0:T(8,128)(2,1)}, u32[]{:S(2)}, u32[]{:S(2)}) %all-to-all-start.1) | async-done | bytes 1572896 | tf_op jit(solution)/shard_map/all_to_all | solution.py:481
  55.7 0.0 copy-done
  55.7 0.0 copy-done.1
  55.7 0.0 copy-done.2
  55.8 24.8 %rest.1 = bf16[4,2,64,384]{3,2,1,0:T(8,128)(2,1)S(1)} custom-call(s32[1,4]{1,0:T(1,128)S(1)} %copy-done, bf16[128,16,384]{2,1,0:T(8,128)(2,1)} %all-to-all-done.1.recv, f32[32,320,384]{2,1,0:T(8,128)} %own.1.acc_in, f32[2,384]{1,0:T(2,128)S(1)} %copy-done.1, f32[2,384]{1,0:T(2,128)S(1)} %copy-done.2, bf16[2,27,384,384]{3,2,1,0:T(8,128)(2,1)} %bitcast.12), custom_call_target="tpu_custom_call" | custom-call | flops 12230590464 | bytes 25165824 | tf_op jit(solution)/shard_map/rest/pallas_call | solution.py:507
  80.5 11.2 %all_to_all.15 = bf16[4,2,64,384]{3,2,1,0:T(8,128)(2,1)S(1)} all-to-all(bf16[4,2,64,384]{3,2,1,0:T(8,128)(2,1)S(1)} %rest.1), channel_id=1, replica_groups=mesh['stretch'=32,'space'=4] {'space'}, dimensions={0} | all-to-all | bytes 786432 | tf_op jit(solution)/shard_map/all_to_all | solution.py:533
  91.7 0.8 fusion
Async XLA Ops:
  3.0 18.8 %all-to-all-start = ((bf16[32,56,128]{2,1,0:T(8,128)(2,1)}), bf16[32,56,128]{2,1,0:T(8,128)(2,1)S(1)}, u32[]{:S(2)}, u32[]{:S(2)}) async-start(bf16[32,56,128]{2,1,0:T(8,128)(2,1)} %get-tuple-element.6), calls=%async_computation | async-start | bytes 917504 | tf_op jit(solution)/shard_map/all_to_all | solution.py:466
  11.2 20.3 %collective-permute-start = (bf16[28,16,384]{2,1,0:T(8,128)(2,1)}, bf16[28,16,384]{2,1,0:T(8,128)(2,1)S(1)}, u32[]{:S(2)}, u32[]{:S(2)}) collective-permute-start(bf16[28,16,384]{2,1,0:T(8,128)(2,1)} %get-tuple-element.7), channel_id=1, source_target_pairs={{0,1},{1,2},{2,3},{3,0},{4,5},{5,6},{6,7},{7,4},{8,9},{9,10},{10,1... | collective-permute-start | bytes 1032200 | tf_op jit(solution)/shard_map/ppermute | solution.py:463
  12.9 18.7 %collective-permute-start.1 = (bf16[28,16,384]{2,1,0:T(8,128)(2,1)}, bf16[28,16,384]{2,1,0:T(8,128)(2,1)S(1)}, u32[]{:S(2)}, u32[]{:S(2)}) collective-permute-start(bf16[28,16,384]{2,1,0:T(8,128)(2,1)} %get-tuple-element.8), channel_id=1, source_target_pairs={{0,2},{1,3},{2,0},{3,1},{4,6},{5,7},{6,4},{7,5},{8,10},{9,11},{10,... | collective-permute-start | bytes 1032200 | tf_op jit(solution)/shard_map/ppermute | solution.py:463
  15.8 15.8 %collective-permute-start.2 = (bf16[28,16,384]{2,1,0:T(8,128)(2,1)}, bf16[28,16,384]{2,1,0:T(8,128)(2,1)S(1)}, u32[]{:S(2)}, u32[]{:S(2)}) collective-permute-start(bf16[28,16,384]{2,1,0:T(8,128)(2,1)} %get-tuple-element.9), channel_id=1, source_target_pairs={{0,3},{1,0},{2,1},{3,2},{4,7},{5,4},{6,5},{7,6},{8,11},{9,8},{10,9... | collective-permute-start | bytes 1032200 | tf_op jit(solution)/shard_map/ppermute | solution.py:463
  24.2 31.6 %all-to-all-start.1 = ((bf16[128,16,384]{2,1,0:T(8,128)(2,1)}), bf16[128,16,384]{2,1,0:T(8,128)(2,1)}, u32[]{:S(2)}, u32[]{:S(2)}) async-start(bf16[128,16,384]{2,1,0:T(8,128)(2,1)} %route.1), calls=%async_computation.1 | async-start | bytes 3145728 | tf_op jit(solution)/shard_map/all_to_all | solution.py:481
  31.6 0.7 copy-start.3
  31.6 0.8 copy-start.4
  31.6 0.9 %copy-start.5 = (bf16[28,16,384]{2,1,0:T(8,128)(2,1)}, bf16[28,16,384]{2,1,0:T(8,128)(2,1)S(1)}, u32[]{:S(2)}) copy-start(bf16[28,16,384]{2,1,0:T(8,128)(2,1)S(1)} %collective-permute-done.2.from3) | copy-start | bytes 1032196
  32.5 23.2 %copy-start = (s32[1,4]{1,0:T(1,128)S(1)}, s32[1,4]{1,0:T(1,128)}, u32[]{:S(2)}) copy-start(s32[1,4]{1,0:T(1,128)} %table.5) | copy-start | bytes 52
  32.5 23.2 %copy-start.1 = (f32[2,384]{1,0:T(2,128)S(1)}, f32[2,384]{1,0:T(2,128)}, u32[]{:S(2)}) copy-start(f32[2,384]{1,0:T(2,128)} %gain.3) | copy-start | bytes 9220
  32.5 23.2 %copy-start.2 = (f32[2,384]{1,0:T(2,128)S(1)}, f32[2,384]{1,0:T(2,128)}, u32[]{:S(2)}) copy-start(f32[2,384]{1,0:T(2,128)} %bias.3) | copy-start | bytes 9220

commit v4 on v3

--- a/solution.py
+++ b/solution.py
@@ -145,21 +145,22 @@
         store_shifted(slab, out_idx, r, s)
         return 0
 
-    lax.fori_loop(0, ROWS, body, 0, unroll=2)
-
-
-def norm_back_sums(x, idx, mean, inv_std, gain, bias, acc, f):
+    lax.fori_loop(0, ROWS, body, 0, unroll=4)
+
+
+def norm_back_sums(x, idx, mean, inv_std, gain, bias, acc, f, share):
     def body(r, tot):
         at = pl.ds(COLS + r * COLS, COLS)
         n = (x[idx, pl.ds(r * COLS, COLS), :].astype(F32) - mean) * inv_std
         v = n * gain + bias
         sig = sigmoid(v)
-        gn = acc[f, at, :] * (sig * (1.0 + v * (1.0 - sig)) * gain)
+        upstream = acc[f, at, :] if share is None else acc[f, at, :] + share[f, at, :]
+        gn = upstream * (sig * (1.0 + v * (1.0 - sig)) * gain)
         acc[f, at, :] = gn
         return tot[0] + fold(gn), tot[1] + fold(gn * n)
 
     zero = jnp.zeros((8, C), F32)
-    one, two = lax.fori_loop(0, ROWS, body, (zero, zero), unroll=2)
+    one, two = lax.fori_loop(0, ROWS, body, (zero, zero), unroll=4)
     return jnp.sum(one, axis=0, keepdims=True), jnp.sum(two, axis=0, keepdims=True)
 
 
@@ -189,8 +190,6 @@
 def wait_weights(weight, taps, sems, layer):
     for copy in layer_weights(weight, taps, sems, layer):
         copy.wait()
-    if layer == 0:
-        start_weights(weight, taps, sems, 1)
 
 
 def prepare_kernel(table, frames, cot, pieces, *windows):
@@ -223,7 +222,7 @@
     return jnp.minimum(7 - g - first, 6) * 4
 
 
-def route_kernel(pieces, out, held, found, links, sem):
+def route_kernel(pieces, out, held, found, links, sorted_blocks, sem, out_sems):
     block = lax.axis_index("stretch")
     g = lax.rem(block, 16) // 4
     raw = block < 16
@@ -241,10 +240,26 @@
         for j in range(4):
             raw_src = jnp.where(j <= g, prv, jnp.where(j >= g + 2, nxt, -1))
             src = jnp.where(raw, raw_src, jnp.where(j >= g, nxt, -1))
-            out[d * 4 + j] = held[jnp.where(src < 0, 32, src)]
-        return 0
-
-    lax.fori_loop(0, 32, body, 0, unroll=4)
+            sorted_blocks[d * 4 + j] = held[jnp.where(src < 0, 32, src)]
+        return 0
+
+    sends = []
+    for part in range(4):
+        lax.fori_loop(part * 8, part * 8 + 8, body, 0, unroll=4)
+        at = pl.ds(part * 32, 32)
+        sends.append(pltpu.make_async_copy(sorted_blocks.at[at], out.at[at], out_sems.at[part]))
+        sends[-1].start()
+    for send in sends:
+        send.wait()
+
+
+def share_copies(src, dst, sems):
+    inner = pl.ds(COLS, CELLS)
+    parts = [(pl.ds(0, 5), inner), (8,), (pl.ds(5, 3), inner), (9, inner)]
+    return [
+        pltpu.make_async_copy(src.at[part], dst.at[part], sems.at[n])
+        for n, part in enumerate(parts)
+    ]
 
 
 def own_kernel(
@@ -270,7 +285,7 @@
             store_shifted(gslab, g, holder * 2 + r, cot.astype(F32))
             return 0
 
-        lax.fori_loop(0, 8, rows, 0)
+        lax.fori_loop(0, 8, rows, 0, unroll=2)
     frame_stats(x, 4, sums, mean, inv_std, ones)
 
     def normed(g, _):
@@ -282,6 +297,7 @@
 
     lax.fori_loop(0, 4, normed, 0)
     wait_weights(weight, taps, sems, 0)
+    start_weights(weight, taps, sems, 1)
 
     def forward(f, _):
         low = jnp.maximum(0, 4 - j - f)
@@ -293,11 +309,9 @@
     acc[8, 0:8] = mean[...]
     acc[8, 8:16] = inv_std[...]
     acc[8, COLS : COLS + CELLS] = x[j].astype(F32)
-    saves = [
-        pltpu.make_async_copy(acc.at[0:5], acc_out.at[0:5], save_sems.at[0]),
-        pltpu.make_async_copy(acc.at[5:10], acc_out.at[5:10], save_sems.at[1]),
-    ]
+    saves = share_copies(acc, acc_out, save_sems)
     saves[0].start()
+    saves[1].start()
     wait_weights(weight, taps, sems, 1)
 
     def backward(f, _):
@@ -323,18 +337,18 @@
         lax.fori_loop(0, 2, normed1, 0)
         by_count(conv_taps, slab, 3 - j, taps.at[1], 4 - j, j - 1, acc, 9)
 
-    saves[1].start()
+    saves[2].start()
+    saves[3].start()
     for save in saves:
         save.wait()
 
 
 def rest_kernel(
     table, recv, acc_in, gain, bias, weight, out,
-    taps, x, slab, gslab, acc, acc2, h, sums, mean, inv_std, ones, sems, load_sem,
+    taps, x, slab, gslab, acc, share, h, sums, mean, inv_std, ones, sems, load_sems,
 ):
-    load = pltpu.make_async_copy(acc_in.at[0:10], acc, load_sem)
-    load.start()
     start_weights(weight, taps, sems, 0)
+    loads = share_copies(acc_in, share, load_sems)
     j = lax.axis_index("space")
     has_prev = (table[0, 3] >= 0).astype(F32)
     ones[...] = group_matrix()
@@ -352,21 +366,32 @@
         store_shifted(gslab, g, row, cot.astype(F32))
         return 0
 
-    lax.fori_loop(0, 32, rows, 0)
+    lax.fori_loop(0, 32, rows, 0, unroll=4)
     frame_stats(x, 4, sums, mean, inv_std, ones)
+    start_weights(weight, taps, sems, 1)
 
     def normed(g, _):
         mask = jnp.where(g >= j, has_prev, 1.0)
-        norm_silu_frame(
-            x, g, mean[pl.ds(g, 1), :], inv_std[pl.ds(g, 1), :],
-            gain[0:1, :], bias[0:1, :], slab, g, mask,
-        )
+
+        @pl.when(g != j - 1)
+        def _():
+            norm_silu_frame(
+                x, g, mean[pl.ds(g, 1), :], inv_std[pl.ds(g, 1), :],
+                gain[0:1, :], bias[0:1, :], slab, g, mask,
+            )
+
         return 0
 
     lax.fori_loop(0, 4, normed, 0)
-    lax.fori_loop(0, 8 * (j + 1), cot_rows, 0)
-    load.wait()
+    def cot_frame(g, _):
+        lax.fori_loop(0, 8, lambda r, _: cot_rows(g * 8 + r, 0), 0, unroll=4)
+        return 0
+
+    lax.fori_loop(0, j + 1, cot_frame, 0)
+    acc[...] = jnp.zeros_like(acc)
     wait_weights(weight, taps, sems, 0)
+    for load in loads:
+        load.start()
 
     def forward(f, _):
         prev = f < 4 - j
@@ -386,8 +411,12 @@
 
     lax.fori_loop(0, 3, backward, 0)
 
+    for load in loads:
+        load.wait()
+
     def rounded(f, _):
-        h[f] = acc[f, COLS : COLS + CELLS, :].astype(BF16)
+        inner = pl.ds(COLS, CELLS)
+        h[f] = (acc[f, inner, :] + share[f, inner, :]).astype(BF16)
         return 0
 
     lax.fori_loop(0, 5, rounded, 0)
@@ -401,17 +430,18 @@
         )
         return 0
 
-    lax.fori_loop(0, 3, normed1, 0)
-    by_count(conv_taps, slab, 0, taps.at[1], 0, jnp.minimum(3, 4 - j), acc, 9)
+    lax.fori_loop(0, jnp.minimum(3, 4 - j), normed1, 0)
+    by_count(conv_taps, slab, 0, taps.at[1], 0, jnp.minimum(3, 4 - j), acc, 8)
     for i in range(4):
-        out[i, 0] = acc[9, COLS + i * 64 : COLS + i * 64 + 64, :].astype(BF16)
+        inner = pl.ds(COLS + i * 64, 64)
+        out[i, 0] = (acc[8, inner, :] + share[9, inner, :]).astype(BF16)
 
     sums[...] = jnp.zeros_like(sums)
 
     def back_sums(f, _):
         n = f + 2
         one, two = norm_back_sums(
-            h, n, mean[pl.ds(n, 1), :], inv_std[pl.ds(n, 1), :], gain1, bias1, acc, 5 + f
+            h, n, mean[pl.ds(n, 1), :], inv_std[pl.ds(n, 1), :], gain1, bias1, acc, 5 + f, share
         )
         sums[pl.ds(f, 1), :] = one
         sums[pl.ds(f + 4, 1), :] = two
@@ -430,19 +460,17 @@
         store_shifted(slab, f, r, g1)
         return 0
 
-    lax.fori_loop(0, 24, back_rows, 0)
-    acc2[...] = jnp.zeros_like(acc2)
-
-    adjoint_taps(slab, 2, taps.at[0], 0, 3, acc2, 0)
-
-    m0, i0 = acc[8, pl.ds(j, 1), :], acc[8, pl.ds(8 + j, 1), :]
-    raw_own = acc.at[8:9, COLS : COLS + CELLS]
-    one, two = norm_back_sums(raw_own, 0, m0, i0, gain[0:1, :], bias[0:1, :], acc2, 0)
+    lax.fori_loop(0, 24, back_rows, 0, unroll=4)
+    adjoint_taps(slab, 2, taps.at[0], 0, 3, acc, 9)
+
+    m0, i0 = share[8, pl.ds(j, 1), :], share[8, pl.ds(8 + j, 1), :]
+    raw_own = share.at[8:9, COLS : COLS + CELLS]
+    one, two = norm_back_sums(raw_own, 0, m0, i0, gain[0:1, :], bias[0:1, :], acc, 9, None)
     sums[0:1, :] = one
     sums[1:2, :] = two
     sums[...] = group_mean(sums[...], ones)
     for r in range(8):
-        g0 = norm_back_row(raw_own, 0, r, m0, i0, acc2, 0, sums[0:1, :], sums[1:2, :])
+        g0 = norm_back_row(raw_own, 0, r, m0, i0, acc, 9, sums[0:1, :], sums[1:2, :])
         out[r // 2, 1, (r % 2) * COLS : (r % 2 + 1) * COLS, :] = g0.astype(BF16)
 
 
@@ -468,12 +496,14 @@
         route_kernel,
         out_shape=jax.ShapeDtypeStruct((128, 16, C), BF16),
         in_specs=[VMEM],
-        out_specs=VMEM,
+        out_specs=HBM,
         scratch_shapes=[
             pltpu.VMEM((33, 16, C), BF16),
             pltpu.VMEM((8, 128), jnp.int32),
             pltpu.SMEM((8, 128), jnp.int32),
+            pltpu.VMEM((128, 16, C), BF16),
             pltpu.SemaphoreType.DMA,
+            pltpu.SemaphoreType.DMA((4,)),
         ],
         compiler_params=small,
         name="route",
@@ -496,7 +526,7 @@
             pltpu.VMEM((8, C), F32),
             pltpu.VMEM((C, C), BF16),
             pltpu.SemaphoreType.DMA((2, 3)),
-            pltpu.SemaphoreType.DMA((2,)),
+            pltpu.SemaphoreType.DMA((4,)),
         ],
         compiler_params=params,
         cost_estimate=pl.CostEstimate(
@@ -515,14 +545,14 @@
             pltpu.VMEM((4, CELLS, 3 * C), BF16),
             pltpu.VMEM((4, CELLS, 3 * C), BF16),
             pltpu.VMEM((10, PADDED, C), F32),
-            pltpu.VMEM((1, PADDED, C), F32),
+            pltpu.VMEM((10, PADDED, C), F32),
             pltpu.VMEM((5, CELLS, C), BF16),
             pltpu.VMEM((8, C), F32),
             pltpu.VMEM((8, C), F32),
             pltpu.VMEM((8, C), F32),
             pltpu.VMEM((C, C), BF16),
             pltpu.SemaphoreType.DMA((2, 3)),
-            pltpu.SemaphoreType.DMA,
+            pltpu.SemaphoreType.DMA((4,)),
         ],
         compiler_params=pltpu.CompilerParams(vmem_limit_bytes=48 * 2**20),
         cost_estimate=pl.CostEstimate(

time: 92.9 us -> 91.2 us (0.982)
  Pallas kernels: 48.2 us -> 46 us
    pallas_call x1, Pallas kernels: 24.8 us -> 23.2 us  [per_device(): pl.pallas_call(rest_kernel, out_shape=jax.ShapeDtypeStruct((4, 2, 64, C),...]
  transfers between devices with their start and end apart: 5 -> 5, of which waited for: 2 -> 3; matrix products, arithmetic and copies ran while one was open for 0% -> 0% of each run, Pallas kernels for 23% -> 23%
where the time goes in v4:
time: 91.2 us; the launch traced here: 90.6 us
  Pallas kernels  46 us (50%)
  starting transfers between devices  21.5 us (24%)
  blocking collectives  11.2 us (12%)
  waiting for transfers between devices  9.52 us (10%)
  local copies, waits for them, and re-layouts  1.65 us (2%)
    pallas_call x1, Pallas kernels, per_device(): pl.pallas_call(rest_kernel, out_shape=jax.ShapeDtypeStruct((4, 2, 64, C),...  23.2 us
    pallas_call x1, Pallas kernels, per_device(): pl.pallas_call(own_kernel, out_shape=jax.ShapeDtypeStruct((32, PADDED, C)...  18.4 us
    all_to_all x1, blocking collectives, per_device(): back = lax.all_to_all(out, 'space', 0, 0, tiled=True)  11.2 us
    all_to_all x1, starting transfers between devices, per_device(): spread = lax.all_to_all(pieces, 'stretch', 0, 0, tiled=True)  8.24 us
    all_to_all x1, starting transfers between devices, per_device(): recv = lax.all_to_all(routed, ('stretch', 'space'), 0, 0, tiled=True)  7.37 us
    ppermute x3, starting transfers between devices, per_device(): lax.ppermute(window, 'space', [(i, (i + k) % 4) for i in range(4)])  5.9 us
    all_to_all x1, waiting for transfers between devices, per_device(): spread = lax.all_to_all(pieces, 'stretch', 0, 0, tiled=True)  4.65 us
    all_to_all x1, waiting for transfers between devices, per_device(): recv = lax.all_to_all(routed, ('stretch', 'space'), 0, 0, tiled=True)  4.5 us
  transfers between devices with their start and end apart: 5, of which 3 were waited for; matrix products, arithmetic and copies ran while one was open for 0% of the time, Pallas kernels for 23%

profile of v4, /device:TPU:0, one launch (start us, length us, event | category | flops | bytes accessed | tf_op | source)
XLA Modules:
  0.0 90.6 jit_solution(2079524568964856472)
XLA Ops:
  0.6 2.4 %prepare.1 = (bf16[32,56,128]{2,1,0:T(8,128)(2,1)}, bf16[28,16,384]{2,1,0:T(8,128)(2,1)}, bf16[28,16,384]{2,1,0:T(8,128)(2,1)}, bf16[28,16,384]{2,1,0:T(8,128)(2,1)}) custom-call(s32[1,4]{1,0:T(1,128)} %table.5, bf16[16,16,384]{2,1,0:T(8,128)(2,1)} %bitcast.5, bf16[16,16,384]{2,1,0:T(8,128)(2,1)} %bitcast.7), custom_call_target="tpu_custom_call" | custom-call | tf_op jit(solution)/shard_map/prepare/pallas_call | solution.py:482
  3.0 8.2 %all-to-all-start = ((bf16[32,56,128]{2,1,0:T(8,128)(2,1)}), bf16[32,56,128]{2,1,0:T(8,128)(2,1)S(1)}, u32[]{:S(2)}, u32[]{:S(2)}) async-start(bf16[32,56,128]{2,1,0:T(8,128)(2,1)} %get-tuple-element.6), calls=%async_computation | async-start | bytes 917504 | tf_op jit(solution)/shard_map/all_to_all | solution.py:494
  11.2 1.6 %collective-permute-start = (bf16[28,16,384]{2,1,0:T(8,128)(2,1)}, bf16[28,16,384]{2,1,0:T(8,128)(2,1)S(1)}, u32[]{:S(2)}, u32[]{:S(2)}) collective-permute-start(bf16[28,16,384]{2,1,0:T(8,128)(2,1)} %get-tuple-element.7), channel_id=1, source_target_pairs={{0,1},{1,2},{2,3},{3,0},{4,5},{5,6},{6,7},{7,4},{8,9},{9,10},{10,1... | collective-permute-start | bytes 1032200 | tf_op jit(solution)/shard_map/ppermute | solution.py:491
  12.9 2.9 %collective-permute-start.1 = (bf16[28,16,384]{2,1,0:T(8,128)(2,1)}, bf16[28,16,384]{2,1,0:T(8,128)(2,1)S(1)}, u32[]{:S(2)}, u32[]{:S(2)}) collective-permute-start(bf16[28,16,384]{2,1,0:T(8,128)(2,1)} %get-tuple-element.8), channel_id=1, source_target_pairs={{0,2},{1,3},{2,0},{3,1},{4,6},{5,7},{6,4},{7,5},{8,10},{9,11},{10,... | collective-permute-start | bytes 1032200 | tf_op jit(solution)/shard_map/ppermute | solution.py:491
  15.8 1.4 %collective-permute-start.2 = (bf16[28,16,384]{2,1,0:T(8,128)(2,1)}, bf16[28,16,384]{2,1,0:T(8,128)(2,1)S(1)}, u32[]{:S(2)}, u32[]{:S(2)}) collective-permute-start(bf16[28,16,384]{2,1,0:T(8,128)(2,1)} %get-tuple-element.9), channel_id=1, source_target_pairs={{0,3},{1,0},{2,1},{3,2},{4,7},{5,4},{6,5},{7,6},{8,11},{9,8},{10,9... | collective-permute-start | bytes 1032200 | tf_op jit(solution)/shard_map/ppermute | solution.py:491
  17.1 4.7 %all-to-all-done.pieces = bf16[32,56,128]{2,1,0:T(8,128)(2,1)S(1)} async-done(((bf16[32,56,128]{2,1,0:T(8,128)(2,1)}), bf16[32,56,128]{2,1,0:T(8,128)(2,1)S(1)}, u32[]{:S(2)}, u32[]{:S(2)}) %all-to-all-start) | async-done | bytes 458784 | tf_op jit(solution)/shard_map/all_to_all | solution.py:494
  21.8 2.0 %route.1 = bf16[128,16,384]{2,1,0:T(8,128)(2,1)} custom-call(bf16[32,56,128]{2,1,0:T(8,128)(2,1)S(1)} %all-to-all-done.pieces), custom_call_target="tpu_custom_call" | custom-call | tf_op jit(solution)/shard_map/route/pallas_call | solution.py:495
  23.8 7.4 %all-to-all-start.1 = ((bf16[128,16,384]{2,1,0:T(8,128)(2,1)}), bf16[128,16,384]{2,1,0:T(8,128)(2,1)}, u32[]{:S(2)}, u32[]{:S(2)}) async-start(bf16[128,16,384]{2,1,0:T(8,128)(2,1)} %route.1), calls=%async_computation.1 | async-start | bytes 3145728 | tf_op jit(solution)/shard_map/all_to_all | solution.py:511
  31.2 0.0 collective-permute-done.from1
  31.2 0.0 copy-start.3
  31.2 0.4 collective-permute-done.1.from2
  31.6 0.0 copy-start.4
  31.6 0.0 collective-permute-done.2.from3
  31.6 0.0 copy-start.5
  31.6 0.4 copy-done.3
  31.9 0.4 copy-done.4
  32.3 0.1 copy-done.5
  32.4 0.0 copy-start
  32.4 0.0 copy-start.1
  32.5 0.0 copy-start.2
  32.5 18.4 %own.1.acc_in = f32[32,320,384]{2,1,0:T(8,128)} custom-call(s32[1,4]{1,0:T(1,128)} %table.5, bf16[16,16,384]{2,1,0:T(8,128)(2,1)} %bitcast.6, bf16[16,16,384]{2,1,0:T(8,128)(2,1)} %bitcast.8, bf16[28,16,384]{2,1,0:T(8,128)(2,1)} %copy-done.3, bf16[28,16,384]{2,1,0:T(8,128)(2,1)} %copy-done.4, bf16[28,16,384]{2,1,0:T(8,128)(2,1)} %copy-done.5, ...), custom_call_target="tpu_custom_call" | custom-call | flops 1019215872000 | bytes 25165824 | tf_op jit(solution)/shard_map/own/pallas_call | solution.py:512
  50.9 4.5 %all-to-all-done.1.recv = bf16[128,16,384]{2,1,0:T(8,128)(2,1)} async-done(((bf16[128,16,384]{2,1,0:T(8,128)(2,1)}), bf16[128,16,384]{2,1,0:T(8,128)(2,1)}, u32[]{:S(2)}, u32[]{:S(2)}) %all-to-all-start.1) | async-done | bytes 1572896 | tf_op jit(solution)/shard_map/all_to_all | solution.py:511
  55.4 0.0 copy-done
  55.4 0.0 copy-done.1
  55.4 0.0 copy-done.2
  55.4 23.2 %rest.1 = bf16[4,2,64,384]{3,2,1,0:T(8,128)(2,1)S(1)} custom-call(s32[1,4]{1,0:T(1,128)S(1)} %copy-done, bf16[128,16,384]{2,1,0:T(8,128)(2,1)} %all-to-all-done.1.recv, f32[32,320,384]{2,1,0:T(8,128)} %own.1.acc_in, f32[2,384]{1,0:T(2,128)S(1)} %copy-done.1, f32[2,384]{1,0:T(2,128)S(1)} %copy-done.2, bf16[2,27,384,384]{3,2,1,0:T(8,128)(2,1)} %bitcast.12), custom_call_target="tpu_custom_call" | custom-call | flops 12230590464 | bytes 25165824 | tf_op jit(solution)/shard_map/rest/pallas_call | solution.py:537
  78.6 11.2 %all_to_all.15 = bf16[4,2,64,384]{3,2,1,0:T(8,128)(2,1)S(1)} all-to-all(bf16[4,2,64,384]{3,2,1,0:T(8,128)(2,1)S(1)} %rest.1), channel_id=1, replica_groups=mesh['stretch'=32,'space'=4] {'space'}, dimensions={0} | all-to-all | bytes 786432 | tf_op jit(solution)/shard_map/all_to_all | solution.py:563
  89.8 0.8 fusion
Async XLA Ops:
  3.0 18.8 %all-to-all-start = ((bf16[32,56,128]{2,1,0:T(8,128)(2,1)}), bf16[32,56,128]{2,1,0:T(8,128)(2,1)S(1)}, u32[]{:S(2)}, u32[]{:S(2)}) async-start(bf16[32,56,128]{2,1,0:T(8,128)(2,1)} %get-tuple-element.6), calls=%async_computation | async-start | bytes 917504 | tf_op jit(solution)/shard_map/all_to_all | solution.py:494
  11.2 20.0 %collective-permute-start = (bf16[28,16,384]{2,1,0:T(8,128)(2,1)}, bf16[28,16,384]{2,1,0:T(8,128)(2,1)S(1)}, u32[]{:S(2)}, u32[]{:S(2)}) collective-permute-start(bf16[28,16,384]{2,1,0:T(8,128)(2,1)} %get-tuple-element.7), channel_id=1, source_target_pairs={{0,1},{1,2},{2,3},{3,0},{4,5},{5,6},{6,7},{7,4},{8,9},{9,10},{10,1... | collective-permute-start | bytes 1032200 | tf_op jit(solution)/shard_map/ppermute | solution.py:491
  12.9 18.7 %collective-permute-start.1 = (bf16[28,16,384]{2,1,0:T(8,128)(2,1)}, bf16[28,16,384]{2,1,0:T(8,128)(2,1)S(1)}, u32[]{:S(2)}, u32[]{:S(2)}) collective-permute-start(bf16[28,16,384]{2,1,0:T(8,128)(2,1)} %get-tuple-element.8), channel_id=1, source_target_pairs={{0,2},{1,3},{2,0},{3,1},{4,6},{5,7},{6,4},{7,5},{8,10},{9,11},{10,... | collective-permute-start | bytes 1032200 | tf_op jit(solution)/shard_map/ppermute | solution.py:491
  15.8 15.8 %collective-permute-start.2 = (bf16[28,16,384]{2,1,0:T(8,128)(2,1)}, bf16[28,16,384]{2,1,0:T(8,128)(2,1)S(1)}, u32[]{:S(2)}, u32[]{:S(2)}) collective-permute-start(bf16[28,16,384]{2,1,0:T(8,128)(2,1)} %get-tuple-element.9), channel_id=1, source_target_pairs={{0,3},{1,0},{2,1},{3,2},{4,7},{5,4},{6,5},{7,6},{8,11},{9,8},{10,9... | collective-permute-start | bytes 1032200 | tf_op jit(solution)/shard_map/ppermute | solution.py:491
  23.8 31.6 %all-to-all-start.1 = ((bf16[128,16,384]{2,1,0:T(8,128)(2,1)}), bf16[128,16,384]{2,1,0:T(8,128)(2,1)}, u32[]{:S(2)}, u32[]{:S(2)}) async-start(bf16[128,16,384]{2,1,0:T(8,128)(2,1)} %route.1), calls=%async_computation.1 | async-start | bytes 3145728 | tf_op jit(solution)/shard_map/all_to_all | solution.py:511
  31.2 0.7 copy-start.3
  31.6 0.7 copy-start.4
  31.6 0.9 copy-start.5
  32.4 22.9 %copy-start = (s32[1,4]{1,0:T(1,128)S(1)}, s32[1,4]{1,0:T(1,128)}, u32[]{:S(2)}) copy-start(s32[1,4]{1,0:T(1,128)} %table.5) | copy-start | bytes 52
  32.4 22.9 %copy-start.1 = (f32[2,384]{1,0:T(2,128)S(1)}, f32[2,384]{1,0:T(2,128)}, u32[]{:S(2)}) copy-start(f32[2,384]{1,0:T(2,128)} %gain.3) | copy-start | bytes 9220
  32.5 22.9 %copy-start.2 = (f32[2,384]{1,0:T(2,128)S(1)}, f32[2,384]{1,0:T(2,128)}, u32[]{:S(2)}) copy-start(f32[2,384]{1,0:T(2,128)} %bias.3) | copy-start | bytes 9220

commit v5 on v4

--- a/solution.py
+++ b/solution.py
@@ -91,12 +91,14 @@
         acc[f, b * COLS : b * COLS + CELLS, :] += y[:, b * C : (b + 1) * C]
 
 
-def by_count(step, slab, first, taps, a, n, acc, f):
+def by_count(step, slab, first, taps, a, n, acc, f, beside=None):
     for count in (1, 2, 3):
 
         @pl.when(n == count)
         def _(count=count):
             step(slab, first, taps, a, count, acc, f)
+            if beside is not None:
+                beside()
 
 
 def frame_sums(x, idx):
@@ -160,7 +162,7 @@
         return tot[0] + fold(gn), tot[1] + fold(gn * n)
 
     zero = jnp.zeros((8, C), F32)
-    one, two = lax.fori_loop(0, ROWS, body, (zero, zero), unroll=4)
+    one, two = lax.fori_loop(0, ROWS, body, (zero, zero), unroll=True)
     return jnp.sum(one, axis=0, keepdims=True), jnp.sum(two, axis=0, keepdims=True)
 
 
@@ -431,37 +433,32 @@
         return 0
 
     lax.fori_loop(0, jnp.minimum(3, 4 - j), normed1, 0)
-    by_count(conv_taps, slab, 0, taps.at[1], 0, jnp.minimum(3, 4 - j), acc, 8)
+
+    def norm_back():
+        sums[...] = jnp.zeros_like(sums)
+        for f in range(3):
+            n = f + 2
+            one, two = norm_back_sums(
+                h, n, mean[n : n + 1, :], inv_std[n : n + 1, :], gain1, bias1, acc, 5 + f, share
+            )
+            sums[f : f + 1, :] = one
+            sums[f + 4 : f + 5, :] = two
+        sums[...] = group_mean(sums[...], ones[...])
+        for f in range(3):
+            n = f + 2
+            for r in range(ROWS):
+                g1 = norm_back_row(
+                    h, n, r, mean[n : n + 1, :], inv_std[n : n + 1, :], acc, 5 + f,
+                    sums[f : f + 1, :], sums[f + 4 : f + 5, :],
+                )
+                store_shifted(gslab, f, r, g1)
+
+    by_count(conv_taps, slab, 0, taps.at[1], 0, jnp.minimum(3, 4 - j), acc, 8, norm_back)
     for i in range(4):
         inner = pl.ds(COLS + i * 64, 64)
         out[i, 0] = (acc[8, inner, :] + share[9, inner, :]).astype(BF16)
 
-    sums[...] = jnp.zeros_like(sums)
-
-    def back_sums(f, _):
-        n = f + 2
-        one, two = norm_back_sums(
-            h, n, mean[pl.ds(n, 1), :], inv_std[pl.ds(n, 1), :], gain1, bias1, acc, 5 + f, share
-        )
-        sums[pl.ds(f, 1), :] = one
-        sums[pl.ds(f + 4, 1), :] = two
-        return 0
-
-    lax.fori_loop(0, 3, back_sums, 0)
-    sums[...] = group_mean(sums[...], ones)
-
-    def back_rows(t, _):
-        f, r = t // 8, lax.rem(t, 8)
-        n = f + 2
-        g1 = norm_back_row(
-            h, n, r, mean[pl.ds(n, 1), :], inv_std[pl.ds(n, 1), :], acc, 5 + f,
-            sums[pl.ds(f, 1), :], sums[pl.ds(f + 4, 1), :],
-        )
-        store_shifted(slab, f, r, g1)
-        return 0
-
-    lax.fori_loop(0, 24, back_rows, 0, unroll=4)
-    adjoint_taps(slab, 2, taps.at[0], 0, 3, acc, 9)
+    adjoint_taps(gslab, 2, taps.at[0], 0, 3, acc, 9)
 
     m0, i0 = share[8, pl.ds(j, 1), :], share[8, pl.ds(8 + j, 1), :]
     raw_own = share.at[8:9, COLS : COLS + CELLS]

time: 91.2 us -> 90.6 us (level)
  no operation moved by 1% of the time
where the time goes in v5:
time: 90.6 us; the launch traced here: 89.9 us
  Pallas kernels  45.4 us (50%)
  starting transfers between devices  21.5 us (24%)
  blocking collectives  11.2 us (12%)
  waiting for transfers between devices  9.52 us (11%)
  local copies, waits for them, and re-layouts  1.65 us (2%)
    pallas_call x1, Pallas kernels, per_device(): pl.pallas_call(rest_kernel, out_shape=jax.ShapeDtypeStruct((4, 2, 64, C),...  22.6 us
    pallas_call x1, Pallas kernels, per_device(): pl.pallas_call(own_kernel, out_shape=jax.ShapeDtypeStruct((32, PADDED, C)...  18.4 us
    all_to_all x1, blocking collectives, per_device(): back = lax.all_to_all(out, 'space', 0, 0, tiled=True)  11.2 us
    all_to_all x1, starting transfers between devices, per_device(): spread = lax.all_to_all(pieces, 'stretch', 0, 0, tiled=True)  8.24 us
    all_to_all x1, starting transfers between devices, per_device(): recv = lax.all_to_all(routed, ('stretch', 'space'), 0, 0, tiled=True)  7.37 us
    ppermute x3, starting transfers between devices, per_device(): lax.ppermute(window, 'space', [(i, (i + k) % 4) for i in range(4)])  5.9 us
    all_to_all x1, waiting for transfers between devices, per_device(): spread = lax.all_to_all(pieces, 'stretch', 0, 0, tiled=True)  4.65 us
    all_to_all x1, waiting for transfers between devices, per_device(): recv = lax.all_to_all(routed, ('stretch', 'space'), 0, 0, tiled=True)  4.5 us
  transfers between devices with their start and end apart: 5, of which 3 were waited for; matrix products, arithmetic and copies ran while one was open for 0% of the time, Pallas kernels for 23%

profile of v5, /device:TPU:0, one launch (start us, length us, event | category | flops | bytes accessed | tf_op | source)
XLA Modules:
  0.0 89.9 jit_solution(1138053549401909758)
XLA Ops:
  0.6 2.4 %prepare.1 = (bf16[32,56,128]{2,1,0:T(8,128)(2,1)}, bf16[28,16,384]{2,1,0:T(8,128)(2,1)}, bf16[28,16,384]{2,1,0:T(8,128)(2,1)}, bf16[28,16,384]{2,1,0:T(8,128)(2,1)}) custom-call(s32[1,4]{1,0:T(1,128)} %table.5, bf16[16,16,384]{2,1,0:T(8,128)(2,1)} %bitcast.5, bf16[16,16,384]{2,1,0:T(8,128)(2,1)} %bitcast.7), custom_call_target="tpu_custom_call" | custom-call | tf_op jit(solution)/shard_map/prepare/pallas_call | solution.py:479
  3.0 8.2 %all-to-all-start = ((bf16[32,56,128]{2,1,0:T(8,128)(2,1)}), bf16[32,56,128]{2,1,0:T(8,128)(2,1)S(1)}, u32[]{:S(2)}, u32[]{:S(2)}) async-start(bf16[32,56,128]{2,1,0:T(8,128)(2,1)} %get-tuple-element.6), calls=%async_computation | async-start | bytes 917504 | tf_op jit(solution)/shard_map/all_to_all | solution.py:491
  11.2 1.6 %collective-permute-start = (bf16[28,16,384]{2,1,0:T(8,128)(2,1)}, bf16[28,16,384]{2,1,0:T(8,128)(2,1)S(1)}, u32[]{:S(2)}, u32[]{:S(2)}) collective-permute-start(bf16[28,16,384]{2,1,0:T(8,128)(2,1)} %get-tuple-element.7), channel_id=1, source_target_pairs={{0,1},{1,2},{2,3},{3,0},{4,5},{5,6},{6,7},{7,4},{8,9},{9,10},{10,1... | collective-permute-start | bytes 1032200 | tf_op jit(solution)/shard_map/ppermute | solution.py:488
  12.9 2.9 %collective-permute-start.1 = (bf16[28,16,384]{2,1,0:T(8,128)(2,1)}, bf16[28,16,384]{2,1,0:T(8,128)(2,1)S(1)}, u32[]{:S(2)}, u32[]{:S(2)}) collective-permute-start(bf16[28,16,384]{2,1,0:T(8,128)(2,1)} %get-tuple-element.8), channel_id=1, source_target_pairs={{0,2},{1,3},{2,0},{3,1},{4,6},{5,7},{6,4},{7,5},{8,10},{9,11},{10,... | collective-permute-start | bytes 1032200 | tf_op jit(solution)/shard_map/ppermute | solution.py:488
  15.8 1.4 %collective-permute-start.2 = (bf16[28,16,384]{2,1,0:T(8,128)(2,1)}, bf16[28,16,384]{2,1,0:T(8,128)(2,1)S(1)}, u32[]{:S(2)}, u32[]{:S(2)}) collective-permute-start(bf16[28,16,384]{2,1,0:T(8,128)(2,1)} %get-tuple-element.9), channel_id=1, source_target_pairs={{0,3},{1,0},{2,1},{3,2},{4,7},{5,4},{6,5},{7,6},{8,11},{9,8},{10,9... | collective-permute-start | bytes 1032200 | tf_op jit(solution)/shard_map/ppermute | solution.py:488
  17.1 4.7 %all-to-all-done.pieces = bf16[32,56,128]{2,1,0:T(8,128)(2,1)S(1)} async-done(((bf16[32,56,128]{2,1,0:T(8,128)(2,1)}), bf16[32,56,128]{2,1,0:T(8,128)(2,1)S(1)}, u32[]{:S(2)}, u32[]{:S(2)}) %all-to-all-start) | async-done | bytes 458784 | tf_op jit(solution)/shard_map/all_to_all | solution.py:491
  21.8 2.0 %route.1 = bf16[128,16,384]{2,1,0:T(8,128)(2,1)} custom-call(bf16[32,56,128]{2,1,0:T(8,128)(2,1)S(1)} %all-to-all-done.pieces), custom_call_target="tpu_custom_call" | custom-call | tf_op jit(solution)/shard_map/route/pallas_call | solution.py:492
  23.8 7.4 %all-to-all-start.1 = ((bf16[128,16,384]{2,1,0:T(8,128)(2,1)}), bf16[128,16,384]{2,1,0:T(8,128)(2,1)}, u32[]{:S(2)}, u32[]{:S(2)}) async-start(bf16[128,16,384]{2,1,0:T(8,128)(2,1)} %route.1), calls=%async_computation.1 | async-start | bytes 3145728 | tf_op jit(solution)/shard_map/all_to_all | solution.py:508
  31.2 0.0 collective-permute-done.from1
  31.2 0.0 copy-start.3
  31.2 0.4 collective-permute-done.1.from2
  31.6 0.0 copy-start.4
  31.6 0.0 collective-permute-done.2.from3
  31.6 0.0 copy-start.5
  31.6 0.4 copy-done.3
  31.9 0.4 copy-done.4
  32.3 0.1 copy-done.5
  32.4 0.0 copy-start
  32.4 0.0 copy-start.1
  32.5 0.0 copy-start.2
  32.5 18.4 %own.1.acc_in = f32[32,320,384]{2,1,0:T(8,128)} custom-call(s32[1,4]{1,0:T(1,128)} %table.5, bf16[16,16,384]{2,1,0:T(8,128)(2,1)} %bitcast.6, bf16[16,16,384]{2,1,0:T(8,128)(2,1)} %bitcast.8, bf16[28,16,384]{2,1,0:T(8,128)(2,1)} %copy-done.3, bf16[28,16,384]{2,1,0:T(8,128)(2,1)} %copy-done.4, bf16[28,16,384]{2,1,0:T(8,128)(2,1)} %copy-done.5, ...), custom_call_target="tpu_custom_call" | custom-call | flops 1019215872000 | bytes 25165824 | tf_op jit(solution)/shard_map/own/pallas_call | solution.py:509
  50.9 4.5 %all-to-all-done.1.recv = bf16[128,16,384]{2,1,0:T(8,128)(2,1)} async-done(((bf16[128,16,384]{2,1,0:T(8,128)(2,1)}), bf16[128,16,384]{2,1,0:T(8,128)(2,1)}, u32[]{:S(2)}, u32[]{:S(2)}) %all-to-all-start.1) | async-done | bytes 1572896 | tf_op jit(solution)/shard_map/all_to_all | solution.py:508
  55.4 0.0 copy-done
  55.4 0.0 copy-done.1
  55.4 0.0 copy-done.2
  55.4 22.6 %rest.1 = bf16[4,2,64,384]{3,2,1,0:T(8,128)(2,1)S(1)} custom-call(s32[1,4]{1,0:T(1,128)S(1)} %copy-done, bf16[128,16,384]{2,1,0:T(8,128)(2,1)} %all-to-all-done.1.recv, f32[32,320,384]{2,1,0:T(8,128)} %own.1.acc_in, f32[2,384]{1,0:T(2,128)S(1)} %copy-done.1, f32[2,384]{1,0:T(2,128)S(1)} %copy-done.2, bf16[2,27,384,384]{3,2,1,0:T(8,128)(2,1)} %bitcast.12), custom_call_target="tpu_custom_call" | custom-call | flops 12230590464 | bytes 25165824 | tf_op jit(solution)/shard_map/rest/pallas_call | solution.py:534
  78.0 11.2 %all_to_all.15 = bf16[4,2,64,384]{3,2,1,0:T(8,128)(2,1)S(1)} all-to-all(bf16[4,2,64,384]{3,2,1,0:T(8,128)(2,1)S(1)} %rest.1), channel_id=1, replica_groups=mesh['stretch'=32,'space'=4] {'space'}, dimensions={0} | all-to-all | bytes 786432 | tf_op jit(solution)/shard_map/all_to_all | solution.py:560
  89.1 0.8 fusion
Async XLA Ops:
  3.0 18.8 %all-to-all-start = ((bf16[32,56,128]{2,1,0:T(8,128)(2,1)}), bf16[32,56,128]{2,1,0:T(8,128)(2,1)S(1)}, u32[]{:S(2)}, u32[]{:S(2)}) async-start(bf16[32,56,128]{2,1,0:T(8,128)(2,1)} %get-tuple-element.6), calls=%async_computation | async-start | bytes 917504 | tf_op jit(solution)/shard_map/all_to_all | solution.py:491
  11.2 20.0 %collective-permute-start = (bf16[28,16,384]{2,1,0:T(8,128)(2,1)}, bf16[28,16,384]{2,1,0:T(8,128)(2,1)S(1)}, u32[]{:S(2)}, u32[]{:S(2)}) collective-permute-start(bf16[28,16,384]{2,1,0:T(8,128)(2,1)} %get-tuple-element.7), channel_id=1, source_target_pairs={{0,1},{1,2},{2,3},{3,0},{4,5},{5,6},{6,7},{7,4},{8,9},{9,10},{10,1... | collective-permute-start | bytes 1032200 | tf_op jit(solution)/shard_map/ppermute | solution.py:488
  12.9 18.7 %collective-permute-start.1 = (bf16[28,16,384]{2,1,0:T(8,128)(2,1)}, bf16[28,16,384]{2,1,0:T(8,128)(2,1)S(1)}, u32[]{:S(2)}, u32[]{:S(2)}) collective-permute-start(bf16[28,16,384]{2,1,0:T(8,128)(2,1)} %get-tuple-element.8), channel_id=1, source_target_pairs={{0,2},{1,3},{2,0},{3,1},{4,6},{5,7},{6,4},{7,5},{8,10},{9,11},{10,... | collective-permute-start | bytes 1032200 | tf_op jit(solution)/shard_map/ppermute | solution.py:488
  15.8 15.8 %collective-permute-start.2 = (bf16[28,16,384]{2,1,0:T(8,128)(2,1)}, bf16[28,16,384]{2,1,0:T(8,128)(2,1)S(1)}, u32[]{:S(2)}, u32[]{:S(2)}) collective-permute-start(bf16[28,16,384]{2,1,0:T(8,128)(2,1)} %get-tuple-element.9), channel_id=1, source_target_pairs={{0,3},{1,0},{2,1},{3,2},{4,7},{5,4},{6,5},{7,6},{8,11},{9,8},{10,9... | collective-permute-start | bytes 1032200 | tf_op jit(solution)/shard_map/ppermute | solution.py:488
  23.8 31.6 %all-to-all-start.1 = ((bf16[128,16,384]{2,1,0:T(8,128)(2,1)}), bf16[128,16,384]{2,1,0:T(8,128)(2,1)}, u32[]{:S(2)}, u32[]{:S(2)}) async-start(bf16[128,16,384]{2,1,0:T(8,128)(2,1)} %route.1), calls=%async_computation.1 | async-start | bytes 3145728 | tf_op jit(solution)/shard_map/all_to_all | solution.py:508
  31.2 0.7 copy-start.3
  31.6 0.7 copy-start.4
  31.6 0.9 copy-start.5
  32.4 22.9 %copy-start = (s32[1,4]{1,0:T(1,128)S(1)}, s32[1,4]{1,0:T(1,128)}, u32[]{:S(2)}) copy-start(s32[1,4]{1,0:T(1,128)} %table.5) | copy-start | bytes 52
  32.4 22.9 %copy-start.1 = (f32[2,384]{1,0:T(2,128)S(1)}, f32[2,384]{1,0:T(2,128)}, u32[]{:S(2)}) copy-start(f32[2,384]{1,0:T(2,128)} %gain.3) | copy-start | bytes 9220
  32.5 22.9 %copy-start.2 = (f32[2,384]{1,0:T(2,128)S(1)}, f32[2,384]{1,0:T(2,128)}, u32[]{:S(2)}) copy-start(f32[2,384]{1,0:T(2,128)} %bias.3) | copy-start | bytes 9220

commit v6 on v5

--- a/solution.py
+++ b/solution.py
@@ -91,8 +91,8 @@
         acc[f, b * COLS : b * COLS + CELLS, :] += y[:, b * C : (b + 1) * C]
 
 
-def by_count(step, slab, first, taps, a, n, acc, f, beside=None):
-    for count in (1, 2, 3):
+def by_count(step, slab, first, taps, a, n, acc, f, beside=None, most=3):
+    for count in range(1, most + 1):
 
         @pl.when(n == count)
         def _(count=count):
@@ -337,7 +337,7 @@
             return 0
 
         lax.fori_loop(0, 2, normed1, 0)
-        by_count(conv_taps, slab, 3 - j, taps.at[1], 4 - j, j - 1, acc, 9)
+        by_count(conv_taps, slab, 3 - j, taps.at[1], 4 - j, j - 1, acc, 9, most=2)
 
     saves[2].start()
     saves[3].start()

time: 90.6 us -> 90.5 us (level)
  no operation moved by 1% of the time
where the time goes in v6:
time: 90.5 us; the launch traced here: 89.9 us
  Pallas kernels  45.3 us (50%)
  starting transfers between devices  21.5 us (24%)
  blocking collectives  11.2 us (12%)
  waiting for transfers between devices  9.56 us (11%)
  local copies, waits for them, and re-layouts  1.65 us (2%)
    pallas_call x1, Pallas kernels, per_device(): pl.pallas_call(rest_kernel, out_shape=jax.ShapeDtypeStruct((4, 2, 64, C),...  22.5 us
    pallas_call x1, Pallas kernels, per_device(): pl.pallas_call(own_kernel, out_shape=jax.ShapeDtypeStruct((32, PADDED, C)...  18.4 us
    all_to_all x1, blocking collectives, per_device(): back = lax.all_to_all(out, 'space', 0, 0, tiled=True)  11.2 us
    all_to_all x1, starting transfers between devices, per_device(): spread = lax.all_to_all(pieces, 'stretch', 0, 0, tiled=True)  8.24 us
    all_to_all x1, starting transfers between devices, per_device(): recv = lax.all_to_all(routed, ('stretch', 'space'), 0, 0, tiled=True)  7.37 us
    ppermute x3, starting transfers between devices, per_device(): lax.ppermute(window, 'space', [(i, (i + k) % 4) for i in range(4)])  5.9 us
    all_to_all x1, waiting for transfers between devices, per_device(): spread = lax.all_to_all(pieces, 'stretch', 0, 0, tiled=True)  4.65 us
    all_to_all x1, waiting for transfers between devices, per_device(): recv = lax.all_to_all(routed, ('stretch', 'space'), 0, 0, tiled=True)  4.54 us
  transfers between devices with their start and end apart: 5, of which 3 were waited for; matrix products, arithmetic and copies ran while one was open for 0% of the time, Pallas kernels for 23%

profile of v6, /device:TPU:0, one launch (start us, length us, event | category | flops | bytes accessed | tf_op | source)
XLA Modules:
  0.0 89.9 jit_solution(3724314699834813014)
XLA Ops:
  0.6 2.4 %prepare.1 = (bf16[32,56,128]{2,1,0:T(8,128)(2,1)}, bf16[28,16,384]{2,1,0:T(8,128)(2,1)}, bf16[28,16,384]{2,1,0:T(8,128)(2,1)}, bf16[28,16,384]{2,1,0:T(8,128)(2,1)}) custom-call(s32[1,4]{1,0:T(1,128)} %table.5, bf16[16,16,384]{2,1,0:T(8,128)(2,1)} %bitcast.5, bf16[16,16,384]{2,1,0:T(8,128)(2,1)} %bitcast.7), custom_call_target="tpu_custom_call" | custom-call | tf_op jit(solution)/shard_map/prepare/pallas_call | solution.py:479
  3.0 8.2 %all-to-all-start = ((bf16[32,56,128]{2,1,0:T(8,128)(2,1)}), bf16[32,56,128]{2,1,0:T(8,128)(2,1)S(1)}, u32[]{:S(2)}, u32[]{:S(2)}) async-start(bf16[32,56,128]{2,1,0:T(8,128)(2,1)} %get-tuple-element.6), calls=%async_computation | async-start | bytes 917504 | tf_op jit(solution)/shard_map/all_to_all | solution.py:491
  11.2 1.6 %collective-permute-start = (bf16[28,16,384]{2,1,0:T(8,128)(2,1)}, bf16[28,16,384]{2,1,0:T(8,128)(2,1)S(1)}, u32[]{:S(2)}, u32[]{:S(2)}) collective-permute-start(bf16[28,16,384]{2,1,0:T(8,128)(2,1)} %get-tuple-element.7), channel_id=1, source_target_pairs={{0,1},{1,2},{2,3},{3,0},{4,5},{5,6},{6,7},{7,4},{8,9},{9,10},{10,1... | collective-permute-start | bytes 1032200 | tf_op jit(solution)/shard_map/ppermute | solution.py:488
  12.9 2.9 %collective-permute-start.1 = (bf16[28,16,384]{2,1,0:T(8,128)(2,1)}, bf16[28,16,384]{2,1,0:T(8,128)(2,1)S(1)}, u32[]{:S(2)}, u32[]{:S(2)}) collective-permute-start(bf16[28,16,384]{2,1,0:T(8,128)(2,1)} %get-tuple-element.8), channel_id=1, source_target_pairs={{0,2},{1,3},{2,0},{3,1},{4,6},{5,7},{6,4},{7,5},{8,10},{9,11},{10,... | collective-permute-start | bytes 1032200 | tf_op jit(solution)/shard_map/ppermute | solution.py:488
  15.8 1.4 %collective-permute-start.2 = (bf16[28,16,384]{2,1,0:T(8,128)(2,1)}, bf16[28,16,384]{2,1,0:T(8,128)(2,1)S(1)}, u32[]{:S(2)}, u32[]{:S(2)}) collective-permute-start(bf16[28,16,384]{2,1,0:T(8,128)(2,1)} %get-tuple-element.9), channel_id=1, source_target_pairs={{0,3},{1,0},{2,1},{3,2},{4,7},{5,4},{6,5},{7,6},{8,11},{9,8},{10,9... | collective-permute-start | bytes 1032200 | tf_op jit(solution)/shard_map/ppermute | solution.py:488
  17.1 4.7 %all-to-all-done.pieces = bf16[32,56,128]{2,1,0:T(8,128)(2,1)S(1)} async-done(((bf16[32,56,128]{2,1,0:T(8,128)(2,1)}), bf16[32,56,128]{2,1,0:T(8,128)(2,1)S(1)}, u32[]{:S(2)}, u32[]{:S(2)}) %all-to-all-start) | async-done | bytes 458784 | tf_op jit(solution)/shard_map/all_to_all | solution.py:491
  21.8 2.0 %route.1 = bf16[128,16,384]{2,1,0:T(8,128)(2,1)} custom-call(bf16[32,56,128]{2,1,0:T(8,128)(2,1)S(1)} %all-to-all-done.pieces), custom_call_target="tpu_custom_call" | custom-call | tf_op jit(solution)/shard_map/route/pallas_call | solution.py:492
  23.8 7.4 %all-to-all-start.1 = ((bf16[128,16,384]{2,1,0:T(8,128)(2,1)}), bf16[128,16,384]{2,1,0:T(8,128)(2,1)}, u32[]{:S(2)}, u32[]{:S(2)}) async-start(bf16[128,16,384]{2,1,0:T(8,128)(2,1)} %route.1), calls=%async_computation.1 | async-start | bytes 3145728 | tf_op jit(solution)/shard_map/all_to_all | solution.py:508
  31.2 0.0 collective-permute-done.from1
  31.2 0.0 copy-start.3
  31.2 0.4 collective-permute-done.1.from2
  31.6 0.0 copy-start.4
  31.6 0.0 collective-permute-done.2.from3
  31.6 0.0 copy-start.5
  31.6 0.4 copy-done.3
  31.9 0.4 copy-done.4
  32.3 0.1 copy-done.5
  32.4 0.0 copy-start
  32.4 0.0 copy-start.1
  32.5 0.0 copy-start.2
  32.5 18.4 %own.1.acc_in = f32[32,320,384]{2,1,0:T(8,128)} custom-call(s32[1,4]{1,0:T(1,128)} %table.5, bf16[16,16,384]{2,1,0:T(8,128)(2,1)} %bitcast.6, bf16[16,16,384]{2,1,0:T(8,128)(2,1)} %bitcast.8, bf16[28,16,384]{2,1,0:T(8,128)(2,1)} %copy-done.3, bf16[28,16,384]{2,1,0:T(8,128)(2,1)} %copy-done.4, bf16[28,16,384]{2,1,0:T(8,128)(2,1)} %copy-done.5, ...), custom_call_target="tpu_custom_call" | custom-call | flops 1019215872000 | bytes 25165824 | tf_op jit(solution)/shard_map/own/pallas_call | solution.py:509
  50.8 4.5 %all-to-all-done.1.recv = bf16[128,16,384]{2,1,0:T(8,128)(2,1)} async-done(((bf16[128,16,384]{2,1,0:T(8,128)(2,1)}), bf16[128,16,384]{2,1,0:T(8,128)(2,1)}, u32[]{:S(2)}, u32[]{:S(2)}) %all-to-all-start.1) | async-done | bytes 1572896 | tf_op jit(solution)/shard_map/all_to_all | solution.py:508
  55.4 0.0 copy-done
  55.4 0.0 copy-done.1
  55.4 0.0 copy-done.2
  55.4 22.5 %rest.1 = bf16[4,2,64,384]{3,2,1,0:T(8,128)(2,1)S(1)} custom-call(s32[1,4]{1,0:T(1,128)S(1)} %copy-done, bf16[128,16,384]{2,1,0:T(8,128)(2,1)} %all-to-all-done.1.recv, f32[32,320,384]{2,1,0:T(8,128)} %own.1.acc_in, f32[2,384]{1,0:T(2,128)S(1)} %copy-done.1, f32[2,384]{1,0:T(2,128)S(1)} %copy-done.2, bf16[2,27,384,384]{3,2,1,0:T(8,128)(2,1)} %bitcast.12), custom_call_target="tpu_custom_call" | custom-call | flops 12230590464 | bytes 25165824 | tf_op jit(solution)/shard_map/rest/pallas_call | solution.py:534
  77.9 11.2 %all_to_all.15 = bf16[4,2,64,384]{3,2,1,0:T(8,128)(2,1)S(1)} all-to-all(bf16[4,2,64,384]{3,2,1,0:T(8,128)(2,1)S(1)} %rest.1), channel_id=1, replica_groups=mesh['stretch'=32,'space'=4] {'space'}, dimensions={0} | all-to-all | bytes 786432 | tf_op jit(solution)/shard_map/all_to_all | solution.py:560
  89.1 0.8 fusion
Async XLA Ops:
  3.0 18.8 %all-to-all-start = ((bf16[32,56,128]{2,1,0:T(8,128)(2,1)}), bf16[32,56,128]{2,1,0:T(8,128)(2,1)S(1)}, u32[]{:S(2)}, u32[]{:S(2)}) async-start(bf16[32,56,128]{2,1,0:T(8,128)(2,1)} %get-tuple-element.6), calls=%async_computation | async-start | bytes 917504 | tf_op jit(solution)/shard_map/all_to_all | solution.py:491
  11.2 20.0 %collective-permute-start = (bf16[28,16,384]{2,1,0:T(8,128)(2,1)}, bf16[28,16,384]{2,1,0:T(8,128)(2,1)S(1)}, u32[]{:S(2)}, u32[]{:S(2)}) collective-permute-start(bf16[28,16,384]{2,1,0:T(8,128)(2,1)} %get-tuple-element.7), channel_id=1, source_target_pairs={{0,1},{1,2},{2,3},{3,0},{4,5},{5,6},{6,7},{7,4},{8,9},{9,10},{10,1... | collective-permute-start | bytes 1032200 | tf_op jit(solution)/shard_map/ppermute | solution.py:488
  12.9 18.7 %collective-permute-start.1 = (bf16[28,16,384]{2,1,0:T(8,128)(2,1)}, bf16[28,16,384]{2,1,0:T(8,128)(2,1)S(1)}, u32[]{:S(2)}, u32[]{:S(2)}) collective-permute-start(bf16[28,16,384]{2,1,0:T(8,128)(2,1)} %get-tuple-element.8), channel_id=1, source_target_pairs={{0,2},{1,3},{2,0},{3,1},{4,6},{5,7},{6,4},{7,5},{8,10},{9,11},{10,... | collective-permute-start | bytes 1032200 | tf_op jit(solution)/shard_map/ppermute | solution.py:488
  15.8 15.8 %collective-permute-start.2 = (bf16[28,16,384]{2,1,0:T(8,128)(2,1)}, bf16[28,16,384]{2,1,0:T(8,128)(2,1)S(1)}, u32[]{:S(2)}, u32[]{:S(2)}) collective-permute-start(bf16[28,16,384]{2,1,0:T(8,128)(2,1)} %get-tuple-element.9), channel_id=1, source_target_pairs={{0,3},{1,0},{2,1},{3,2},{4,7},{5,4},{6,5},{7,6},{8,11},{9,8},{10,9... | collective-permute-start | bytes 1032200 | tf_op jit(solution)/shard_map/ppermute | solution.py:488
  23.8 31.6 %all-to-all-start.1 = ((bf16[128,16,384]{2,1,0:T(8,128)(2,1)}), bf16[128,16,384]{2,1,0:T(8,128)(2,1)}, u32[]{:S(2)}, u32[]{:S(2)}) async-start(bf16[128,16,384]{2,1,0:T(8,128)(2,1)} %route.1), calls=%async_computation.1 | async-start | bytes 3145728 | tf_op jit(solution)/shard_map/all_to_all | solution.py:508
  31.2 0.7 copy-start.3
  31.6 0.7 copy-start.4
  31.6 0.9 copy-start.5
  32.4 22.9 %copy-start = (s32[1,4]{1,0:T(1,128)S(1)}, s32[1,4]{1,0:T(1,128)}, u32[]{:S(2)}) copy-start(s32[1,4]{1,0:T(1,128)} %table.5) | copy-start | bytes 52
  32.4 22.9 %copy-start.1 = (f32[2,384]{1,0:T(2,128)S(1)}, f32[2,384]{1,0:T(2,128)}, u32[]{:S(2)}) copy-start(f32[2,384]{1,0:T(2,128)} %gain.3) | copy-start | bytes 9220
  32.5 22.9 %copy-start.2 = (f32[2,384]{1,0:T(2,128)S(1)}, f32[2,384]{1,0:T(2,128)}, u32[]{:S(2)}) copy-start(f32[2,384]{1,0:T(2,128)} %bias.3) | copy-start | bytes 9220
